TPU v7x, 128 devices: a whole 4x4x4 slice. The times are simulated.
128 devices in a mesh: fsdp: 8 (over y, x_lo), ctx: 4 (over x_hi, core), tp: 4 (over z).
Axes of the slice: x: 4 (x_hi: 2, x_lo: 2; x = x_hi * 2 + x_lo), y: 4, z: 4, core: 2. Of those that a mesh axis runs over, the one named last changes fastest.
Arguments:
- tokens: bfloat16 [8, 2048, 2048], P('fsdp', 'ctx'), may hold values from -6 to 6
- ln_gain: bfloat16 [2048], P('fsdp'), may hold values from 0.5 to 1.5
- ln_shift: bfloat16 [2048], P('fsdp'), may hold values from -1.75 to 1.75
- out_bias: bfloat16 [2048], P('fsdp'), may hold values from -3 to 3
- w_qkv: bfloat16 [2048, 3, 2048], P('fsdp', None, 'tp'), may hold values from -0.125 to 0.125
- b_qkv: bfloat16 [3, 32, 64], P(None, 'tp', 'fsdp'), may hold values from -1.75 to 1.75
- w_out: bfloat16 [2048, 2048], P('tp', 'fsdp'), may hold values from -0.5 to 0.5
- w_fc1: bfloat16 [2048, 8192], P('fsdp', 'tp'), may hold values from -0.125 to 0.125
- b_fc1: bfloat16 [128, 64], P('tp', 'fsdp'), may hold values from -1.75 to 1.75
- w_fc2: bfloat16 [8192, 2048], P('tp', 'fsdp'), may hold values from -0.0625 to 0.0625
- out_grad: bfloat16 [8, 2048, 2048], P('fsdp', 'ctx'), may hold values from -8 to 8
Outputs:
- layer_out: bfloat16 [8, 2048, 2048], P('fsdp', 'ctx')
- input_grad: bfloat16 [8, 2048, 2048], P('fsdp', 'ctx')
- ln_gain_grad: float32 [2048], P('fsdp')
- ln_shift_grad: float32 [2048], P('fsdp')
- out_bias_grad: float32 [2048], P('fsdp')
- qkv_grad: float32 [2048, 3, 2048], P('fsdp', None, 'tp')
- qkv_bias_grad: float32 [3, 32, 64], P(None, 'tp', 'fsdp')
- out_proj_grad: float32 [2048, 2048], P('tp', 'fsdp')
- fc1_grad: float32 [2048, 8192], P('fsdp', 'tp')
- fc1_bias_grad: float32 [128, 64], P('tp', 'fsdp')
- fc2_grad: float32 [8192, 2048], P('tp', 'fsdp')
All inputs are finite; a program needn't handle non-finite values.
Results may differ from a plain program's by a relative error of at most 0.024.
Values may be sent and summed in bfloat16 or wider, within the bound.
A program may use at most 256 MiB of HBM per device.

v0:
```python
import math

import jax
import jax.numpy as jnp
from jax import lax
from jax.sharding import PartitionSpec as P

H = 32
HD = 64
ROT = 32
FF = 8192


EPSILON = 1e-05
MASKED_SCORE = -1e30


def rope_tables(positions, rot_dims):
    half_dims = rot_dims // 2
    frequency = 10000.0 ** (-2.0 * jnp.arange(half_dims, dtype=jnp.float32) / rot_dims)
    angles = positions.astype(jnp.float32)[:, None] * frequency[None, :]
    return (jnp.cos(angles), jnp.sin(angles))


def rotate(vector, cosine, sine_part, rot_dims, direction):
    half_dims = rot_dims // 2
    first_half = vector[..., :half_dims]
    second_half = vector[..., half_dims:rot_dims]
    remainder = vector[..., rot_dims:]
    cos_rows = cosine[:, None, :]
    sin_rows = sine_part[:, None, :] * direction
    return jnp.concatenate(
        [
            first_half * cos_rows - second_half * sin_rows,
            second_half * cos_rows + first_half * sin_rows,
            remainder,
        ],
        axis=-1,
    )


def attention_scores(queries_low, keys_full, causal_mask, score_scale):
    scores = (
        jnp.einsum("qhd,khd->hqk", queries_low, keys_full, preferred_element_type=jnp.float32)
        * score_scale
    )
    return jnp.where(causal_mask[None], scores, MASKED_SCORE)


def body(tokens, ln_gain, ln_shift, out_bias, w_qkv, b_qkv, w_out, w_fc1, b_fc1, w_fc2, out_grad):
    local_heads = H // lax.axis_size("tp")
    local_width = local_heads * HD
    local_ff = FF // lax.axis_size("tp")
    score_scale = 1.0 / math.sqrt(HD)
    (
        gain_full,
        shift_full,
        bias_full,
        qkv_full,
        qkv_bias_full,
        proj_full,
        up_full,
        up_bias_full,
        down_full,
    ) = (
        lax.all_gather(ln_gain, "fsdp", axis=0, tiled=True),
        lax.all_gather(ln_shift, "fsdp", axis=0, tiled=True),
        lax.all_gather(out_bias, "fsdp", axis=0, tiled=True),
        lax.all_gather(w_qkv, "fsdp", axis=0, tiled=True),
        lax.all_gather(b_qkv, "fsdp", axis=2, tiled=True),
        lax.all_gather(w_out, "fsdp", axis=1, tiled=True),
        lax.all_gather(w_fc1, "fsdp", axis=0, tiled=True),
        lax.all_gather(b_fc1, "fsdp", axis=1, tiled=True),
        lax.all_gather(w_fc2, "fsdp", axis=1, tiled=True),
    )
    inputs = tokens[0].astype(jnp.float32)
    row_count = inputs.shape[0]
    row_mean = jnp.mean(inputs, axis=-1, keepdims=True)
    centered = inputs - row_mean
    inv_std = lax.rsqrt(jnp.mean(centered * centered, axis=-1, keepdims=True) + EPSILON)
    unit_rows = centered * inv_std
    normed_low = (
        unit_rows * gain_full.astype(jnp.float32) + shift_full.astype(jnp.float32)
    ).astype(jnp.bfloat16)
    raw_qkv = jnp.einsum(
        "td,dcf->tcf", normed_low, qkv_full, preferred_element_type=jnp.float32
    ) + qkv_bias_full.astype(jnp.float32).reshape(3, local_width)
    positions = lax.axis_index("ctx") * row_count + jnp.arange(row_count, dtype=jnp.int32)
    cosine, sine_part = rope_tables(positions, ROT)
    head_shape = (row_count, local_heads, HD)
    queries_low = rotate(raw_qkv[:, 0].reshape(head_shape), cosine, sine_part, ROT, 1.0).astype(
        jnp.bfloat16
    )
    keys_low = rotate(raw_qkv[:, 1].reshape(head_shape), cosine, sine_part, ROT, 1.0).astype(
        jnp.bfloat16
    )
    values_low = raw_qkv[:, 2].astype(jnp.bfloat16)
    keys_flat, values_flat = (
        lax.all_gather(keys_low.reshape(row_count, local_width), "ctx", axis=0, tiled=True),
        lax.all_gather(values_low, "ctx", axis=0, tiled=True),
    )
    key_count = keys_flat.shape[0]
    keys_full = keys_flat.reshape(key_count, local_heads, HD)
    values_full = values_flat.reshape(key_count, local_heads, HD)
    causal_mask = jnp.arange(key_count, dtype=jnp.int32)[None, :] <= positions[:, None]
    scores = attention_scores(queries_low, keys_full, causal_mask, score_scale)
    row_max = jnp.max(scores, axis=-1, keepdims=True)
    exp_scores = jnp.exp(scores - row_max)
    exp_total = jnp.sum(exp_scores, axis=-1, keepdims=True)
    probability = exp_scores / exp_total
    log_total = row_max + jnp.log(exp_total)
    attended_low = (
        jnp.einsum(
            "hqk,khd->qhd",
            probability.astype(jnp.bfloat16),
            values_full,
            preferred_element_type=jnp.float32,
        )
        .reshape(row_count, local_width)
        .astype(jnp.bfloat16)
    )
    hidden = jnp.dot(normed_low, up_full, preferred_element_type=jnp.float32) + up_bias_full.astype(
        jnp.float32
    ).reshape(local_ff)
    active_low = jax.nn.gelu(hidden, approximate=True).astype(jnp.bfloat16)
    partial_branch = jnp.dot(attended_low, proj_full, preferred_element_type=jnp.float32) + jnp.dot(
        active_low, down_full, preferred_element_type=jnp.float32
    )
    branch = lax.psum(partial_branch.astype(jnp.bfloat16), "tp").astype(jnp.float32)
    layer_out = (inputs + branch + bias_full.astype(jnp.float32)).astype(jnp.bfloat16)
    gain_back, qkv_back, proj_back, up_back, down_back = (
        lax.all_gather(ln_gain, "fsdp", axis=0, tiled=True),
        lax.all_gather(w_qkv, "fsdp", axis=0, tiled=True),
        lax.all_gather(w_out, "fsdp", axis=1, tiled=True),
        lax.all_gather(w_fc1, "fsdp", axis=0, tiled=True),
        lax.all_gather(w_fc2, "fsdp", axis=1, tiled=True),
    )
    grad_low = out_grad[0]
    grad_rows = grad_low.astype(jnp.float32)
    bias_grad = jnp.sum(grad_rows, axis=0)
    proj_grad = jnp.einsum("tf,td->fd", attended_low, grad_low, preferred_element_type=jnp.float32)
    down_grad = jnp.einsum("tf,td->fd", active_low, grad_low, preferred_element_type=jnp.float32)
    attended_grad = jnp.einsum(
        "td,fd->tf", grad_low, proj_back, preferred_element_type=jnp.float32
    ).astype(jnp.bfloat16)
    active_grad = jnp.einsum("td,fd->tf", grad_low, down_back, preferred_element_type=jnp.float32)
    gelu_pull = jax.vjp(lambda values_in: jax.nn.gelu(values_in, approximate=True), hidden)[1]
    hidden_grad = gelu_pull(active_grad)[0].astype(jnp.bfloat16)
    up_bias_grad = jnp.sum(hidden_grad.astype(jnp.float32), axis=0).reshape(local_ff // HD, HD)
    up_grad = jnp.einsum("td,tf->df", normed_low, hidden_grad, preferred_element_type=jnp.float32)
    normed_grad = jnp.einsum("tf,df->td", hidden_grad, up_back, preferred_element_type=jnp.float32)
    scores = attention_scores(queries_low, keys_full, causal_mask, score_scale)
    probability = jnp.exp(scores - log_total)
    grad_heads = attended_grad.reshape(row_count, local_heads, HD)
    prob_grad = jnp.einsum(
        "qhd,khd->hqk", grad_heads, values_full, preferred_element_type=jnp.float32
    )
    row_dot = jnp.sum(probability * prob_grad, axis=-1, keepdims=True)
    score_grad = (probability * (prob_grad - row_dot)).astype(jnp.bfloat16)
    query_grad = (
        jnp.einsum("hqk,khd->qhd", score_grad, keys_full, preferred_element_type=jnp.float32)
        * score_scale
    )
    key_part = (
        jnp.einsum("hqk,qhd->khd", score_grad, queries_low, preferred_element_type=jnp.float32)
        * score_scale
    )
    value_part = jnp.einsum(
        "hqk,qhd->khd",
        probability.astype(jnp.bfloat16),
        grad_heads,
        preferred_element_type=jnp.float32,
    )
    key_back, value_back = (
        lax.psum_scatter(
            key_part.reshape(key_count, local_width).astype(jnp.bfloat16),
            "ctx",
            scatter_dimension=0,
            tiled=True,
        ).astype(jnp.float32),
        lax.psum_scatter(
            value_part.reshape(key_count, local_width).astype(jnp.bfloat16),
            "ctx",
            scatter_dimension=0,
            tiled=True,
        ).astype(jnp.float32),
    )
    query_raw = rotate(query_grad, cosine, sine_part, ROT, -1.0).reshape(row_count, local_width)
    key_raw = rotate(key_back.reshape(head_shape), cosine, sine_part, ROT, -1.0).reshape(
        row_count, local_width
    )
    raw_grad = jnp.stack([query_raw, key_raw, value_back], axis=1).astype(jnp.bfloat16)
    qkv_bias_grad = jnp.sum(raw_grad.astype(jnp.float32), axis=0).reshape(3, local_heads, HD)
    qkv_grad = jnp.einsum("td,tcf->dcf", normed_low, raw_grad, preferred_element_type=jnp.float32)
    normed_grad = normed_grad + jnp.einsum(
        "tcf,dcf->td", raw_grad, qkv_back, preferred_element_type=jnp.float32
    )
    normed_total = lax.psum(normed_grad.astype(jnp.bfloat16), "tp").astype(jnp.float32)
    gain_grad = jnp.sum(normed_total * unit_rows, axis=0)
    shift_grad = jnp.sum(normed_total, axis=0)
    scaled_grad = normed_total * gain_back.astype(jnp.float32)
    input_rows = inv_std * (
        scaled_grad
        - jnp.mean(scaled_grad, axis=-1, keepdims=True)
        - unit_rows * jnp.mean(scaled_grad * unit_rows, axis=-1, keepdims=True)
    )
    input_total = (input_rows + grad_rows).astype(jnp.bfloat16)
    pieces = (
        lax.psum_scatter(
            gain_grad.astype(jnp.bfloat16), ("fsdp", "ctx"), scatter_dimension=0, tiled=True
        ).astype(jnp.float32),
        lax.psum_scatter(
            shift_grad.astype(jnp.bfloat16), ("fsdp", "ctx"), scatter_dimension=0, tiled=True
        ).astype(jnp.float32),
        lax.psum_scatter(
            bias_grad.astype(jnp.bfloat16), ("fsdp", "ctx"), scatter_dimension=0, tiled=True
        ).astype(jnp.float32),
        lax.psum_scatter(
            qkv_grad.astype(jnp.bfloat16), ("fsdp", "ctx"), scatter_dimension=0, tiled=True
        ).astype(jnp.float32),
        lax.psum_scatter(
            qkv_bias_grad.astype(jnp.bfloat16), ("fsdp", "ctx"), scatter_dimension=2, tiled=True
        ).astype(jnp.float32),
        lax.psum_scatter(
            proj_grad.astype(jnp.bfloat16), ("fsdp", "ctx"), scatter_dimension=1, tiled=True
        ).astype(jnp.float32),
        lax.psum_scatter(
            up_grad.astype(jnp.bfloat16), ("fsdp", "ctx"), scatter_dimension=0, tiled=True
        ).astype(jnp.float32),
        lax.psum_scatter(
            up_bias_grad.astype(jnp.bfloat16), ("fsdp", "ctx"), scatter_dimension=1, tiled=True
        ).astype(jnp.float32),
        lax.psum_scatter(
            down_grad.astype(jnp.bfloat16), ("fsdp", "ctx"), scatter_dimension=1, tiled=True
        ).astype(jnp.float32),
    )
    owned_grads = (
        lax.all_gather(pieces[0].astype(jnp.bfloat16), "ctx", axis=0, tiled=True).astype(
            jnp.float32
        ),
        lax.all_gather(pieces[1].astype(jnp.bfloat16), "ctx", axis=0, tiled=True).astype(
            jnp.float32
        ),
        lax.all_gather(pieces[2].astype(jnp.bfloat16), "ctx", axis=0, tiled=True).astype(
            jnp.float32
        ),
        lax.all_gather(pieces[3].astype(jnp.bfloat16), "ctx", axis=0, tiled=True).astype(
            jnp.float32
        ),
        lax.all_gather(pieces[4].astype(jnp.bfloat16), "ctx", axis=2, tiled=True).astype(
            jnp.float32
        ),
        lax.all_gather(pieces[5].astype(jnp.bfloat16), "ctx", axis=1, tiled=True).astype(
            jnp.float32
        ),
        lax.all_gather(pieces[6].astype(jnp.bfloat16), "ctx", axis=0, tiled=True).astype(
            jnp.float32
        ),
        lax.all_gather(pieces[7].astype(jnp.bfloat16), "ctx", axis=1, tiled=True).astype(
            jnp.float32
        ),
        lax.all_gather(pieces[8].astype(jnp.bfloat16), "ctx", axis=1, tiled=True).astype(
            jnp.float32
        ),
    )
    return (
        layer_out[None],
        input_total[None],
        owned_grads[0],
        owned_grads[1],
        owned_grads[2],
        owned_grads[3],
        owned_grads[4],
        owned_grads[5],
        owned_grads[6],
        owned_grads[7],
        owned_grads[8],
    )


def solution(mesh):
    in_specs = (
        P("fsdp", "ctx", None),
        P("fsdp"),
        P("fsdp"),
        P("fsdp"),
        P("fsdp", None, "tp"),
        P(None, "tp", "fsdp"),
        P("tp", "fsdp"),
        P("fsdp", "tp"),
        P("tp", "fsdp"),
        P("tp", "fsdp"),
        P("fsdp", "ctx", None),
    )
    out_specs = (
        P("fsdp", "ctx", None),
        P("fsdp", "ctx", None),
        P("fsdp"),
        P("fsdp"),
        P("fsdp"),
        P("fsdp", None, "tp"),
        P(None, "tp", "fsdp"),
        P("tp", "fsdp"),
        P("fsdp", "tp"),
        P("tp", "fsdp"),
        P("tp", "fsdp"),
    )
    return jax.shard_map(body, mesh=mesh, in_specs=in_specs, out_specs=out_specs, check_vma=False)
```

profile of v0, /device:TPU:1, one launch (start us, length us, event | category | flops | bytes accessed | tf_op | source)
XLA Modules:
  0.0 1435.0 jit_solution(12888075949616837844)
XLA Ops:
  11.1 16.5 %all-gather.1 = bf16[8,1,256]{2,1,0:T(2,128)(2,1)S(1)} all-gather(bf16[1,1,256]{2,1,0:T(2,128)(2,1)S(1)} %reshape.209), channel_id=1, replica_groups=mesh['fsdp'=8,'ctx'=4,'tp'=4] {'fsdp'}, dimensions={0}, use_global_device_ids=true | all-gather | bytes 4608 | tf_op jit(solution)/shard_map/all_gather | solution.py:66
  28.3 12.5 all-gather.2
  41.6 23.4 %all_gather.68 = bf16[3,8,64]{1,0,2:T(4,128)(2,1)S(1)} all-gather(bf16[3,8,8]{1,0,2:T(4,128)(2,1)S(1)} %copy.81), channel_id=1, replica_groups=mesh['fsdp'=8,'ctx'=4,'tp'=4] {'fsdp'}, dimensions={2}, use_global_device_ids=true | all-gather | bytes 3456 | tf_op jit(solution)/shard_map/all_gather | solution.py:70
  67.1 76.4 %all-gather.14.cloned.1.call-done = bf16[2048,3,512]{0,2,1:T(8,128)(2,1)} async-done(((bf16[256,3,512]{0,2,1:T(8,128)(2,1)}), bf16[2048,3,512]{0,2,1:T(8,128)(2,1)}) %all-gather.14.cloned.1.call-update) | async-done | bytes 6291472 | tf_op jit(solution)/shard_map/all_gather | solution.py:69
  143.5 5.9 fusion.50
  156.8 39.7 %all-gather.18.cloned.1.call-done = bf16[512,2048]{1,0:T(8,128)(2,1)} async-done(((bf16[512,256]{1,0:T(8,128)(2,1)}), bf16[512,2048]{1,0:T(8,128)(2,1)}) %all-gather.18.cloned.1.call-update) | async-done | bytes 2097168 | tf_op jit(solution)/shard_map/all_gather | solution.py:71
  196.5 4.3 fusion.54
  201.8 25.6 %all-gather.16.cloned.1.call-done = bf16[2048,512]{0,1:T(8,128)(2,1)} async-done(((bf16[512,512]{0,1:T(8,128)(2,1)}), bf16[2048,512]{0,1:T(8,128)(2,1)}) %all-gather.16.cloned.1.call-update) | async-done | bytes 2097168 | tf_op jit(solution)/shard_map/all_gather | solution.py:99
  227.4 16.0 %fusion.69 = (f32[8,512]{1,0:T(8,128)S(1)}, f32[8,512,2048]{2,1,0:T(8,128)}) fusion(bf16[2048,8,64]{0,2,1:T(8,128)(2,1)} %bitcast.140, bf16[512,8,32]{0,2,1:T(8,128)(2,1)S(1)} %slice.103, bf16[512,8,16]{0,2,1:T(8,128)(2,1)} %get-tuple-element.99, bf16[512,8,16]{0,2,1:T(8,128)(2,1)S(1)} %get-tuple-element.98, pred[512,2048]{1,0:T(8,128)(4,1)S(1)} %iota_compare_fusion), kind=kOutput, calls=%fused_computation.108 | convolution fusion | flops 1100476416 | bytes 37240832 | tf_op jit(solution)/shard_map/qhd,khd->hqk/dot_general | solution.py:44
  243.4 13.7 fusion
  257.2 23.0 %multiply_reduce_fusion = (f32[8,512]{1,0:T(8,128)S(1)}, f32[8,512,2048]{2,1,0:T(8,128)}) fusion(f32[8,512,2048]{2,1,0:T(8,128)} %get-tuple-element.110, f32[8,512]{1,0:T(8,128)S(1)} %log_add_fusion, bf16[512,8,64]{0,2,1:T(8,128)(2,1)S(1)} %bitcast.143, bf16[2048,8,64]{0,2,1:T(8,128)(2,1)} %bitcast.149), kind=kOutput, calls=%fused_computation.1 | convolution fusion | flops 1098903552 | bytes 69763072 | tf_op jit(solution)/shard_map/qhd,khd->hqk/dot_general | solution.py:155
  280.2 28.1 %multiply_convert_fusion = bf16[8,512,2048]{2,1,0:T(8,128)(2,1)} fusion(f32[8,512,2048]{2,1,0:T(8,128)} %get-tuple-element.112, f32[8,512,2048]{2,1,0:T(8,128)} %get-tuple-element.110, f32[8,512]{1,0:T(8,128)S(1)} %get-tuple-element.111, f32[8,512]{1,0:T(8,128)S(1)} %log_add_fusion), kind=kLoop, calls=%fused_computation | loop fusion | flops 33554432 | bytes 83918848 | tf_op jit(solution)/shard_map/convert_element_type | solution.py:159
  308.4 10.2 multiply_convert_fusion.1
  318.7 21.0 %all_gather.73 = bf16[32,64]{0,1:T(8,128)(2,1)S(1)} all-gather(bf16[32,8]{0,1:T(8,128)(2,1)S(1)} %copy-done.20), channel_id=1, replica_groups=mesh['fsdp'=8,'ctx'=4,'tp'=4] {'fsdp'}, dimensions={1}, use_global_device_ids=true | all-gather | bytes 4608 | tf_op jit(solution)/shard_map/all_gather | solution.py:73
  339.9 15.0 %fusion.34 = bf16[8,64,2048]{2,1,0:T(8,128)(2,1)} fusion(bf16[512,8,64]{0,2,1:T(8,128)(2,1)S(1)} %bitcast.144, f32[8,512,2048]{2,1,0:T(8,128)} %get-tuple-element.110, f32[8,512]{1,0:T(8,128)S(1)} %log_add_fusion), kind=kOutput, calls=%fused_computation.53 | convolution fusion | flops 1091567616 | bytes 36192256 | tf_op jit(solution)/shard_map/hqk,qhd->khd/dot_general | solution.py:168
  354.9 4.0 copy.84
  358.9 65.9 %all-gather.20.cloned.1.call-done = bf16[2048,2048]{1,0:T(8,128)(2,1)} async-done(((bf16[256,2048]{1,0:T(8,128)(2,1)}), bf16[2048,2048]{1,0:T(8,128)(2,1)}) %all-gather.20.cloned.1.call-update) | async-done | bytes 8388624 | tf_op jit(solution)/shard_map/all_gather | solution.py:72
  424.8 9.6 fusion.65
  434.4 160.9 %all-gather.22.cloned.1.call-done = bf16[2048,2048]{1,0:T(8,128)(2,1)} async-done(((bf16[2048,256]{1,0:T(8,128)(2,1)}), bf16[2048,2048]{1,0:T(8,128)(2,1)}) %all-gather.22.cloned.1.call-update) | async-done | bytes 8388624 | tf_op jit(solution)/shard_map/all_gather | solution.py:74
  595.4 12.1 fusion.70
  608.8 7.2 convolution_convert_fusion.1
  616.3 11.7 fusion.53
  628.0 15.3 %fusion.57 = bf16[8,64,512]{2,1,0:T(8,128)(2,1)} fusion(bf16[2048,8,64]{0,2,1:T(8,128)(2,1)} %bitcast.150, f32[8,512,2048]{2,1,0:T(8,128)} %get-tuple-element.110, f32[8,512]{1,0:T(8,128)S(1)} %copy-done.13, f32[8,512]{1,0:T(8,128)S(1)} %get-tuple-element.109), kind=kOutput, calls=%fused_computation.71 | convolution fusion | flops 1099169792 | bytes 36208640 | tf_op jit(solution)/shard_map/hqk,khd->qhd/dot_general | solution.py:113
  643.3 4.4 convolution_convert_fusion.3
  647.9 9.9 fusion.62
  657.9 2.7 add_convert_fusion
  660.6 9.7 fusion.71
  674.9 4.2 reduce-scatter.10.cloned.1.call-done
  679.1 8.9 fusion.33
  688.3 11.0 convolution_convert_fusion
  699.4 6.8 convolution_convert_fusion.2
  706.3 125.3 %reduce-scatter.16.cloned.1.call-done = bf16[64,2048]{1,0:T(8,128)(2,1)} async-done(((bf16[2048,2048]{1,0:T(8,128)(2,1)}), bf16[64,2048]{1,0:T(8,128)(2,1)}) %reduce-scatter.16.cloned.1.call-update) | async-done | bytes 262160 | tf_op jit(solution)/shard_map/reduce_scatter | solution.py:227
  835.6 12.2 all-gather.3
  850.7 122.4 %reduce-scatter.14.cloned.1.call-done = bf16[512,64]{0,1:T(8,128)(2,1)} async-done(((bf16[512,2048]{0,1:T(8,128)(2,1)}), bf16[512,64]{0,1:T(8,128)(2,1)}) %reduce-scatter.14.cloned.1.call-update) | async-done | bytes 65552 | tf_op jit(solution)/shard_map/reduce_scatter | solution.py:224
  973.1 12.5 all_gather.81
  986.6 85.6 %all-reduce.13.cloned.1.call-done = (bf16[512,2048]{1,0:T(8,128)(2,1)}, bf16[512,2048]{1,0:T(8,128)(2,1)}) async-done(((bf16[512,2048]{1,0:T(8,128)(2,1)}, bf16[512,2048]{1,0:T(8,128)(2,1)}), (bf16[512,2048]{1,0:T(8,128)(2,1)}, bf16[512,2048]{1,0:T(8,128)(2,1)})) %all-reduce.13.cloned.1.call-update) | async-done | bytes 4194320 | tf_op jit(solution)/shard_map/psum | solution.py:198
  1074.2 3.5 fusion.25
  1077.7 128.3 %all-reduce.8 = (bf16[3,8,64]{1,0,2:T(4,128)(2,1)S(1)}, bf16[2048]{0:T(1024)(128)(2,1)S(1)}, bf16[2048]{0:T(1024)(128)(2,1)S(1)}, bf16[2048]{0:T(1024)(128)(2,1)S(1)}, bf16[32,64]{1,0:T(8,128)(2,1)S(1)}) all-reduce(bf16[3,8,64]{1,0,2:T(4,128)(2,1)S(1)} %copy.89, ...), channel_id=9, replica_groups=mesh['fsdp'=8,'ctx'=4,'tp'=4] {'fsdp','ctx'}, use_global_device_ids=true, to_apply=%region_19.20.clone | all-reduce | flops 9728 | bytes 38912
  1206.0 24.1 %reduce-scatter.18.cloned.1.call-done = bf16[2048,64]{0,1:T(8,128)(2,1)} async-done(((bf16[2048,2048]{0,1:T(8,128)(2,1)}), bf16[2048,64]{0,1:T(8,128)(2,1)}) %reduce-scatter.18.cloned.1.call-update) | async-done | bytes 262160 | tf_op jit(solution)/shard_map/reduce_scatter | solution.py:233
  1230.2 12.7 all_gather.80
  1244.5 6.7 all-reduce.10
  1253.0 7.7 all-gather.4
  1261.2 5.8 fusion.38
  1267.0 110.4 %reduce-scatter.12.cloned.1.call-done = bf16[64,3,512]{2,0,1:T(8,128)(2,1)} async-done(((bf16[2048,3,512]{2,0,1:T(8,128)(2,1)}), bf16[64,3,512]{2,0,1:T(8,128)(2,1)}) %reduce-scatter.12.cloned.1.call-update) | async-done | bytes 196624 | tf_op jit(solution)/shard_map/reduce_scatter | solution.py:218
  1377.4 13.9 all_gather.79
  1392.7 11.0 all-gather.24.cloned.1.call-done
  1403.7 2.8 convert_element_type.223
  1406.5 19.0 %all-gather.26.cloned.1.call-done = bf16[2048,256]{0,1:T(8,128)(2,1)} async-done(((bf16[2048,64]{0,1:T(8,128)(2,1)}), bf16[2048,256]{0,1:T(8,128)(2,1)}) %all-gather.26.cloned.1.call-update) | async-done | bytes 1048592 | tf_op jit(solution)/shard_map/all_gather | solution.py:262
  (149 shorter events, 38.7 us)
Async XLA Ops:
  7.2 58.0 %copy-start = (bf16[1,512,2048]{2,1,0:T(8,128)(2,1)S(1)}, bf16[1,512,2048]{2,1,0:T(8,128)(2,1)}, u32[]{:S(2)}) copy-start(bf16[1,512,2048]{2,1,0:T(8,128)(2,1)} %param.11) | copy-start | bytes 6291460
  7.2 136.3 %all-gather.14.cloned.1.call-start = ((), (), s32[]{:S(2)}) async-start(), calls=%async_computation.6 | async-start | bytes 7077888 | tf_op jit(solution)/shard_map/all_gather | solution.py:69
  9.7 186.8 %all-gather.18.cloned.1.call-start = ((), (), s32[]{:S(2)}) async-start(), calls=%async_computation.8 | async-start | bytes 2359296 | tf_op jit(solution)/shard_map/all_gather | solution.py:71
  10.4 217.0 %all-gather.16.cloned.1.call-start = ((), (), s32[]{:S(2)}) async-start(), calls=%async_computation.7 | async-start | bytes 2621440 | tf_op jit(solution)/shard_map/all_gather | solution.py:99
  27.7 121.8 %copy-start.10 = (f32[8,1,256]{2,1,0:T(1,128)}, f32[8,1,256]{2,1,0:T(1,128)S(1)}, u32[]{:S(2)}) copy-start(f32[8,1,256]{2,1,0:T(1,128)S(1)} %convert_element_type.228) | copy-start | bytes 24580
  40.8 108.6 %copy-start.18 = (f32[8,1,256]{2,1,0:T(1,128)}, f32[8,1,256]{2,1,0:T(1,128)S(1)}, u32[]{:S(2)}) copy-start(f32[8,1,256]{2,1,0:T(1,128)S(1)} %convert_element_type.229) | copy-start | bytes 24580
  65.6 83.9 %copy-start.14 = (f32[512]{0:T(512)}, f32[512]{0:T(512)S(1)}, u32[]{:S(2)}) copy-start(f32[512]{0:T(512)S(1)} %broadcast_multiply_fusion.3) | copy-start | bytes 6148
  66.3 83.2 %copy-start.16 = (f32[512]{0:T(512)}, f32[512]{0:T(512)S(1)}, u32[]{:S(2)}) copy-start(f32[512]{0:T(512)S(1)} %add_rsqrt_fusion) | copy-start | bytes 6148
  67.1 82.6 %copy-start.7 = (f32[512,16]{0,1:T(8,128)}, f32[512,16]{0,1:T(8,128)S(1)}, u32[]{:S(2)}) copy-start(f32[512,16]{0,1:T(8,128)S(1)} %get-tuple-element.108) | copy-start | bytes 98308
  149.5 2.2 copy-start.3
  149.7 1.1 copy-start.2
  152.5 104.7 %all-gather.28.cloned.1.call-start = ((), (), s32[]{:S(2)}) async-start(), calls=%async_computation.19 | async-start | bytes 2621440 | tf_op jit(solution)/shard_map/all_gather | solution.py:100
  154.7 270.2 %all-gather.20.cloned.1.call-start = ((), (), s32[]{:S(2)}) async-start(), calls=%async_computation.9 | async-start | bytes 9437184 | tf_op jit(solution)/shard_map/all_gather | solution.py:72
  155.2 440.1 %all-gather.22.cloned.1.call-start = ((), (), s32[]{:S(2)}) async-start(), calls=%async_computation.10 | async-start | bytes 9437184 | tf_op jit(solution)/shard_map/all_gather | solution.py:74
  155.8 514.4 %reduce-scatter.8.cloned.1.call-start = ((), (), s32[]{:S(2)}) async-start(), calls=%async_computation.11 | async-start | bytes 2621440 | tf_op jit(solution)/shard_map/reduce_scatter | solution.py:175
  243.4 13.8 copy-start.1
  257.2 23.1 %copy-start.12 = (f32[8,512]{1,0:T(8,128)}, f32[8,512]{1,0:T(8,128)S(1)}, u32[]{:S(2)}) copy-start(f32[8,512]{1,0:T(8,128)S(1)} %fusion) | copy-start | bytes 49156
  280.2 28.1 %copy-start.5 = (bf16[512,8,16]{0,2,1:T(8,128)(2,1)S(1)}, bf16[512,8,16]{0,2,1:T(8,128)(2,1)}, u32[]{:S(2)}) copy-start(bf16[512,8,16]{0,2,1:T(8,128)(2,1)} %get-tuple-element.99) | copy-start | bytes 393220
  308.4 10.3 copy-start.20
  318.6 360.5 %reduce-scatter.10.cloned.1.call-start = ((), (), s32[]{:S(2)}) async-start(), calls=%async_computation.12 | async-start | bytes 2621440 | tf_op jit(solution)/shard_map/reduce_scatter | solution.py:181
  354.9 69.9 %copy-start.11 = (f32[8,1,256]{2,1,0:T(1,128)S(1)}, f32[8,1,256]{2,1,0:T(1,128)}, u32[]{:S(2)}) copy-start(f32[8,1,256]{2,1,0:T(1,128)} %copy-done.10) | copy-start | bytes 24580
  354.9 69.9 %copy-start.15 = (f32[512]{0:T(512)S(1)}, f32[512]{0:T(512)}, u32[]{:S(2)}) copy-start(f32[512]{0:T(512)} %copy-done.14) | copy-start | bytes 6148
  354.9 69.9 %copy-start.17 = (f32[512]{0:T(512)S(1)}, f32[512]{0:T(512)}, u32[]{:S(2)}) copy-start(f32[512]{0:T(512)} %copy-done.16) | copy-start | bytes 6148
  354.9 69.9 %copy-start.19 = (f32[8,1,256]{2,1,0:T(1,128)S(1)}, f32[8,1,256]{2,1,0:T(1,128)}, u32[]{:S(2)}) copy-start(f32[8,1,256]{2,1,0:T(1,128)} %copy-done.18) | copy-start | bytes 24580
  358.9 472.8 %reduce-scatter.16.cloned.1.call-start = ((), (), s32[]{:S(2)}) async-start(), calls=%async_computation.15 | async-start | bytes 8650752 | tf_op jit(solution)/shard_map/reduce_scatter | solution.py:227
  607.5 1.3 copy-start.24
  616.0 11.9 copy-start.13
  616.0 357.1 %reduce-scatter.14.cloned.1.call-start = ((), (), s32[]{:S(2)}) async-start(), calls=%async_computation.14 | async-start | bytes 2162688 | tf_op jit(solution)/shard_map/reduce_scatter | solution.py:224
  647.7 424.6 %all-reduce.13.cloned.1.call-start = ((), (), s32[]{:S(2)}) async-start(), calls=%async_computation.20 | async-start | bytes 8388608 | tf_op jit(solution)/shard_map/psum | solution.py:198
  647.9 10.0 copy-start.4
  647.9 10.0 copy-start.6
  657.9 2.7 copy-start.25
  660.6 11.8 copy-start.8
  660.6 11.8 copy-start.9
  688.0 542.1 %reduce-scatter.18.cloned.1.call-start = ((), (), s32[]{:S(2)}) async-start(), calls=%async_computation.17 | async-start | bytes 8650752 | tf_op jit(solution)/shard_map/reduce_scatter | solution.py:233
  699.4 678.0 %reduce-scatter.12.cloned.1.call-start = ((), (), s32[]{:S(2)}) async-start(), calls=%async_computation.13 | async-start | bytes 6488064 | tf_op jit(solution)/shard_map/reduce_scatter | solution.py:218
  706.2 127.5 %copy-start.23 = (u32[128]{0:T(128)S(1)}, u32[128]{0:T(128)}, u32[]{:S(2)}) copy-start(u32[128]{0:T(128)} %constant.73) | copy-start | bytes 1540
  706.2 129.4 %copy-start.21 = (bf16[256]{0:T(256)(128)(2,1)S(1)}, bf16[256]{0:T(256)(128)(2,1)}, u32[]{:S(2)}) copy-start(bf16[256]{0:T(256)(128)(2,1)} %param.14) | copy-start | bytes 1540
  706.2 141.6 %copy-start.22 = (u32[128]{0:T(128)S(1)}, u32[128]{0:T(128)}, u32[]{:S(2)}) copy-start(u32[128]{0:T(128)} %constant.55) | copy-start | bytes 1540
  706.2 697.5 %all-gather.24.cloned.1.call-start = ((), (), s32[]{:S(2)}) async-start(), calls=%async_computation.16 | async-start | bytes 1310720 | tf_op jit(solution)/shard_map/all_gather | solution.py:256
  831.7 593.8 %all-gather.26.cloned.1.call-start = ((), (), s32[]{:S(2)}) async-start(), calls=%async_computation.18 | async-start | bytes 1310720 | tf_op jit(solution)/shard_map/all_gather | solution.py:262
Sparse Core Ops, SparseCore 0:
  10.2 133.3 all-gather.13
  145.1 51.3 all-gather.17
  198.7 28.6 all-gather.15
  229.5 26.0 all-gather.27
  257.1 167.6 all-gather.19
  426.2 169.0 all-gather.21
  598.6 39.3 reduce-scatter.7
  641.3 37.7 reduce-scatter.9
  681.5 150.0 reduce-scatter.15
  833.9 139.2 reduce-scatter.13
  976.8 95.3 all-reduce.12
  1074.5 155.5 reduce-scatter.17
  1232.5 144.8 reduce-scatter.11
  1378.9 24.7 all-gather.23
  1405.2 20.1 all-gather.25
where the time goes:
time: 1440 us
  waiting for transfers between devices  873 us (61%)
  blocking collectives  267 us (19%)
  matrix products  184 us (13%)
  other arithmetic  69.3 us (5%)
  local copies, waits for them, and re-layouts  23.9 us (2%)
  between operations  16.9 us (1%)
    all_gather x1, waiting for transfers between devices, body(): lax.all_gather(w_fc2, 'fsdp', axis=1, tiled=True)  161 us
    unnamed x2, blocking collectives  135 us
    reduce_scatter x1, waiting for transfers between devices, body(): lax.psum_scatter(up_grad.astype(jnp.bfloat16), ('fsdp', 'ctx'), scatter_d...  125 us
    reduce_scatter x1, waiting for transfers between devices, body(): lax.psum_scatter(proj_grad.astype(jnp.bfloat16), ('fsdp', 'ctx'), scatter...  122 us
    reduce_scatter x1, waiting for transfers between devices, body(): lax.psum_scatter(qkv_grad.astype(jnp.bfloat16), ('fsdp', 'ctx'), scatter_...  110 us
    psum x1, waiting for transfers between devices, body(): lax.psum(normed_grad.astype(jnp.bfloat16), 'tp').astype(jnp.float32)  85.6 us
    all_gather x1, waiting for transfers between devices, body(): lax.all_gather(w_qkv, 'fsdp', axis=0, tiled=True)  76.4 us
    all_gather x1, waiting for transfers between devices, body(): lax.all_gather(w_fc1, 'fsdp', axis=0, tiled=True)  65.9 us
  transfers between devices with their start and end apart: 15, of which 13 were waited for; matrix products, arithmetic and copies ran while one was open for 19% of the time, Pallas kernels for 0%

commit v1 on v0

v1 whole, which is shorter than its diff:
```python
import functools
import math

import jax
import jax.numpy as jnp
from jax import lax
from jax.experimental import pallas as pl
from jax.experimental.pallas import tpu as pltpu
from jax.sharding import PartitionSpec as P

D = 2048
HD = 64
ROT = 32
BLK = 256
ROWS = 1024
HALF = 512
EPSILON = 1e-05
MASKED = -1e30
F32 = jnp.float32
BF16 = jnp.bfloat16
VMEM_LIMIT = 56 * 1024 * 1024


def params(**kw):
    return pltpu.CompilerParams(vmem_limit_bytes=VMEM_LIMIT, **kw)


def whole():
    return pl.BlockSpec(memory_space=pltpu.VMEM)


def cost(flops, nbytes, trans=0):
    return pl.CostEstimate(flops=int(flops), bytes_accessed=int(nbytes), transcendentals=int(trans))


def plane(arr, dx=0, dy=0, flip=0):
    pairs = []
    for f in range(8):
        for c in range(4):
            x, y, core = (c // 2) * 2 + f % 2, f // 2, c % 2
            x2, y2, core2 = (x + dx) % 4, (y + dy) % 4, core ^ flip
            pairs.append((f * 4 + c, (y2 * 2 + x2 % 2) * 4 + (x2 // 2) * 2 + core2))
    return lax.ppermute(arr, ("fsdp", "ctx"), pairs)


def across(arr, low_to_high):
    pairs = []
    for f in range(8):
        for core in range(2):
            a, b = f * 4 + core, f * 4 + 2 + core
            pairs.append((a, b) if low_to_high else (b, a))
    return lax.ppermute(arr, ("fsdp", "ctx"), pairs)


def along_z(arr, dz):
    return lax.ppermute(arr, "tp", [(i, (i + dz) % 4) for i in range(4)])


def gather_weight(shard):
    r3, r1, r2 = plane(shard, dy=1), plane(shard, dy=-1), plane(shard, dy=2)
    s0 = plane(shard, dx=1)
    s1, s2, s3 = plane(r1, dx=1), plane(r2, dx=-1), plane(r3, dx=-1)
    return jnp.concatenate([shard, r1, r2, r3, s0, s1, s2, s3], axis=0)


def add_low(*parts):
    total = parts[0].astype(F32)
    for part in parts[1:]:
        total = total + part.astype(F32)
    return total.astype(BF16)


def reduce_x_first(block):
    low, high = block(4, 2), block(6, 2)
    r01, r23 = plane(low, dx=1), plane(high, dx=-1)
    a1 = add_low(block(1, 1), r01[BLK:])
    a3 = add_low(block(3, 1), r23[BLK:])
    a2 = add_low(block(2, 1), r23[:BLK])
    t1, t3, t2 = plane(a1, dy=1), plane(a3, dy=-1), plane(a2, dy=2)
    mine = add_low(block(0, 1), r01[:BLK], t1, t3, t2)
    return add_low(mine, plane(mine, dx=2))


def reduce_y_first(block):
    near = [block(1, 1), block(5, 1)]
    far = [block(3, 1), block(7, 1)]
    mid = [block(2, 1), block(6, 1)]
    t1 = [plane(v, dy=1) for v in near]
    t3 = [plane(v, dy=-1) for v in far]
    t2 = [plane(v, dy=2) for v in mid]
    other = add_low(block(4, 1), t1[1], t3[1], t2[1])
    lo, hi = plane(other[: BLK // 2], dx=1), plane(other[BLK // 2 :], dx=-1)
    mine = add_low(block(0, 1), t1[0], t3[0], t2[0], jnp.concatenate([lo, hi], axis=0))
    return add_low(mine, plane(mine, dx=2))


def block_order(y, x_lo, j):
    dx, dy = j // 4, j % 4
    return lax.rem(y + dy, 4) * 2 + lax.rem(x_lo + dx, 2)


def prep_kernel(place, tok, grad, gain, shift, normed, normed_t, unit, grad_rel, grad_t, bias_grad, full, full_u):
    y, x_lo = place[0], place[1]
    rows = tok[...].astype(F32)
    mean = jnp.mean(rows, axis=-1, keepdims=True)
    centered = rows - mean
    inv = lax.rsqrt(jnp.mean(centered * centered, axis=-1, keepdims=True) + EPSILON)
    unit_rows = centered * inv
    full_u[...] = unit_rows
    full[...] = unit_rows * gain[...] + shift[...]

    @pl.when(pl.program_id(0) == 0)
    def _():
        bias_grad[...] = jnp.zeros_like(bias_grad)

    for j in range(8):
        src = pl.ds(pl.multiple_of(block_order(y, x_lo, j) * BLK, BLK), BLK)
        dst = pl.ds(j * BLK, BLK)
        part = full[:, src]
        normed[:, dst] = part.astype(BF16)
        normed_t[dst, :] = part.T.astype(BF16)
        unit[:, dst] = full_u[:, src].astype(BF16)
        g = grad[:, src]
        g32 = g.astype(F32)
        grad_rel[:, dst] = g
        grad_t[dst, :] = g32.T.astype(BF16)
        bias_grad[:, dst] += jnp.sum(g32, axis=0, keepdims=True)


def prep(place, tok, grad, gain, shift):
    tile = 256
    rows = pl.BlockSpec((tile, D), lambda i, p: (i, 0))
    cols = pl.BlockSpec((D, tile), lambda i, p: (0, i))
    vec = pl.BlockSpec((1, D), lambda i, p: (0, 0))
    return pl.pallas_call(
        prep_kernel,
        grid_spec=pltpu.PrefetchScalarGridSpec(
            num_scalar_prefetch=1,
            grid=(ROWS // tile,),
            in_specs=[rows, rows, vec, vec],
            out_specs=[rows, cols, rows, rows, cols, vec],
            scratch_shapes=[pltpu.VMEM((tile, D), F32), pltpu.VMEM((tile, D), F32)],
        ),
        out_shape=[
            jax.ShapeDtypeStruct((ROWS, D), BF16),
            jax.ShapeDtypeStruct((D, ROWS), BF16),
            jax.ShapeDtypeStruct((ROWS, D), BF16),
            jax.ShapeDtypeStruct((ROWS, D), BF16),
            jax.ShapeDtypeStruct((D, ROWS), BF16),
            jax.ShapeDtypeStruct((1, D), F32),
        ],
        compiler_params=params(),
        cost_estimate=cost(40 * ROWS * D, 14 * ROWS * D),
        name="prep",
    )(place, tok, grad, gain, shift)


def partner(v):
    lane = lax.broadcasted_iota(jnp.int32, v.shape, 1)
    up = pltpu.roll(v, v.shape[1] - ROT // 2, 1)
    down = pltpu.roll(v, ROT // 2, 1)
    return jnp.where(lane % HD < ROT // 2, up, down)


def qkv_kernel(normed, grad, w, bias, cos, sin, q, kv, do):
    raw = jnp.dot(normed[...], w[:, : 3 * BLK], preferred_element_type=F32) + bias[...]
    c, s = cos[...], sin[...]
    qr, kr = raw[:, :BLK], raw[:, BLK : 2 * BLK]
    q[...] = ((qr * c + partner(qr) * s).astype(BF16).astype(F32) * (HD**-0.5)).astype(BF16)
    kv[:, :BLK] = (kr * c + partner(kr) * s).astype(BF16)
    kv[:, BLK:] = raw[:, 2 * BLK :].astype(BF16)
    do[...] = jnp.dot(grad[...], w[:, 3 * BLK :], preferred_element_type=F32).astype(BF16)


def qkv_call(normed, grad, w, bias, cos, sin):
    tile = 256
    rows = lambda n: pl.BlockSpec((tile, n), lambda i: (i, 0))
    fixed = lambda a, b: pl.BlockSpec((a, b), lambda i: (0, 0))
    return pl.pallas_call(
        qkv_kernel,
        grid=(ROWS // tile,),
        in_specs=[rows(D), rows(D), fixed(D, 4 * BLK), fixed(1, 3 * BLK), rows(BLK), rows(BLK)],
        out_specs=[rows(BLK), rows(2 * BLK), rows(BLK)],
        out_shape=[
            jax.ShapeDtypeStruct((ROWS, BLK), BF16),
            jax.ShapeDtypeStruct((ROWS, 2 * BLK), BF16),
            jax.ShapeDtypeStruct((ROWS, BLK), BF16),
        ],
        compiler_params=params(),
        cost_estimate=cost(2 * ROWS * D * 4 * BLK, 16 * ROWS * D),
        name="qkv",
    )(normed, grad, w, bias, cos, sin)


QT = 512
KC = 512


def attention_kernel(place, q, kv, kvr, do, cos, sin, cos_r, sin_r, att, dq, dkv, dkvr, keys, vals, keys_t, vals_t, st, dp,
                     p_all, ds_all, qm, dom, out_t, dq_t, dk, dv):
    x_hi = place[2]
    nt = (((1,), (1,)), ((), ()))

    def place_keys(at, src):
        keys[at : at + ROWS, :] = src[:, :BLK]
        vals[at : at + ROWS, :] = src[:, BLK:]
        keys_t[:, at : at + ROWS] = src[:, :BLK].astype(F32).T.astype(BF16)
        vals_t[:, at : at + ROWS] = src[:, BLK:].astype(F32).T.astype(BF16)

    @pl.when(x_hi == 1)
    def _():
        place_keys(0, kvr)
        place_keys(ROWS, kv)

    @pl.when(x_hi == 0)
    def _():
        place_keys(0, kv)

    dk[...] = jnp.zeros_like(dk)
    dv[...] = jnp.zeros_like(dv)
    heads = BLK // HD
    for t in range(ROWS // QT):
        rows = pl.ds(t * QT, QT)
        chunks = x_hi * (ROWS // KC) + (t + 1) * (QT // KC)

        @pl.loop(0, heads)
        def _(h):
            lane = lax.broadcasted_iota(jnp.int32, (QT, BLK), 1) // HD
            mine = lane == h
            hrows = pl.ds(pl.multiple_of(h * HD, HD), HD)
            stack = pl.ds(pl.multiple_of(h * QT, QT), QT)
            qm[stack, :] = jnp.where(mine, q[rows, :], jnp.zeros((), BF16))
            dom[stack, :] = jnp.where(mine, do[rows, :], jnp.zeros((), BF16))

            def score(j, top, masked):
                at = pl.ds(pl.multiple_of(j * KC, KC), KC)
                s = lax.dot_general(keys[at, :], qm[stack, :], nt, preferred_element_type=F32)
                if masked:
                    ki = lax.broadcasted_iota(jnp.int32, (KC, QT), 0)
                    qi = lax.broadcasted_iota(jnp.int32, (KC, QT), 1)
                    s = jnp.where(ki <= qi, s, MASKED)
                st[at, :] = s
                return jnp.maximum(top, jnp.max(s, axis=0, keepdims=True))

            top = lax.fori_loop(0, chunks - 1, lambda j, m: score(j, m, False), jnp.full((1, QT), MASKED, F32))
            top = score(chunks - 1, top, True)

            def weigh(j, carry):
                total, dot = carry
                at = pl.ds(pl.multiple_of(j * KC, KC), KC)
                p = jnp.exp(st[at, :] - top)
                st[at, :] = p
                d = lax.dot_general(vals[at, :], dom[stack, :], nt, preferred_element_type=F32)
                dp[at, :] = d
                return total + jnp.sum(p, axis=0, keepdims=True), dot + jnp.sum(p * d, axis=0, keepdims=True)

            zero = jnp.zeros((1, QT), F32)
            total, dot = lax.fori_loop(0, chunks, weigh, (zero, zero))
            inv = 1.0 / total
            delta = dot * inv
            out_t[hrows, :] = jnp.zeros((HD, QT), F32)
            dq_t[hrows, :] = jnp.zeros((HD, QT), F32)

            def spread(j, _):
                at = pl.ds(pl.multiple_of(j * KC, KC), KC)
                p = st[at, :] * inv
                low = p.astype(BF16)
                ds = (p * (dp[at, :] - delta)).astype(BF16)
                p_all[at, stack] = low
                ds_all[at, stack] = ds
                out_t[hrows, :] += jnp.dot(vals_t[hrows, at], low, preferred_element_type=F32)
                dq_t[hrows, :] += jnp.dot(keys_t[hrows, at], ds, preferred_element_type=F32)
                return 0

            lax.fori_loop(0, chunks, spread, 0)

        def gather(j, _):
            at = pl.ds(pl.multiple_of(j * KC, KC), KC)
            dv[at, :] += jnp.dot(p_all[at, :], dom[...], preferred_element_type=F32)
            dk[at, :] += jnp.dot(ds_all[at, :], qm[...], preferred_element_type=F32)
            return 0

        lax.fori_loop(0, chunks, gather, 0)
        att[rows, :] = out_t[...].T.astype(BF16)
        dqr = dq_t[...].T * (HD**-0.5)
        dq[rows, :] = (dqr * cos[rows, :] - partner(dqr) * sin[rows, :]).astype(BF16)

    def back(at, c, s):
        k = dk[at : at + ROWS, :]
        return k * c[...] - partner(k) * s[...]

    @pl.when(x_hi == 1)
    def _():
        dkv[:, :BLK] = back(ROWS, cos, sin)
        dkv[:, BLK:] = dv[ROWS:, :]
        dkvr[:, :BLK] = back(0, cos_r, sin_r).astype(BF16)
        dkvr[:, BLK:] = dv[:ROWS, :].astype(BF16)

    @pl.when(x_hi == 0)
    def _():
        dkv[:, :BLK] = back(0, cos, sin)
        dkv[:, BLK:] = dv[:ROWS, :]
        dkvr[...] = jnp.zeros_like(dkvr)


def attention(place, q, kv, kvr, do, cos, sin, cos_r, sin_r):
    heads = BLK // HD
    return pl.pallas_call(
        attention_kernel,
        grid_spec=pltpu.PrefetchScalarGridSpec(
            num_scalar_prefetch=1,
            grid=(1,),
            in_specs=[whole()] * 8,
            out_specs=[whole()] * 4,
            scratch_shapes=[
                pltpu.VMEM((2 * ROWS, BLK), BF16),
                pltpu.VMEM((2 * ROWS, BLK), BF16),
                pltpu.VMEM((BLK, 2 * ROWS), BF16),
                pltpu.VMEM((BLK, 2 * ROWS), BF16),
                pltpu.VMEM((2 * ROWS, QT), F32),
                pltpu.VMEM((2 * ROWS, QT), F32),
                pltpu.VMEM((2 * ROWS, heads * QT), BF16),
                pltpu.VMEM((2 * ROWS, heads * QT), BF16),
                pltpu.VMEM((heads * QT, BLK), BF16),
                pltpu.VMEM((heads * QT, BLK), BF16),
                pltpu.VMEM((BLK, QT), F32),
                pltpu.VMEM((BLK, QT), F32),
                pltpu.VMEM((2 * ROWS, BLK), F32),
                pltpu.VMEM((2 * ROWS, BLK), F32),
            ],
        ),
        out_shape=[
            jax.ShapeDtypeStruct((ROWS, BLK), BF16),
            jax.ShapeDtypeStruct((ROWS, BLK), BF16),
            jax.ShapeDtypeStruct((ROWS, 2 * BLK), F32),
            jax.ShapeDtypeStruct((ROWS, 2 * BLK), BF16),
        ],
        compiler_params=params(),
        cost_estimate=cost(2 * 6 * 4 * BLK * 1.5 * ROWS * ROWS, 12 * 1024 * 1024, 8 * ROWS * ROWS),
        name="attention",
    )(place, q, kv, kvr, do, cos, sin, cos_r, sin_r)


GELU_C = math.sqrt(2.0 / math.pi)


def fc1_kernel(normed, w, bias, active, slope):
    v = jnp.dot(normed[...], w[...], preferred_element_type=F32) + bias[...]
    sq = v * v
    t = jnp.tanh(GELU_C * v * (1.0 + 0.044715 * sq))
    half = 0.5 * (1.0 + t)
    active[...] = (v * half).astype(BF16)
    slope[...] = (half + 0.5 * v * (1.0 - t * t) * (GELU_C * (1.0 + 3 * 0.044715 * sq))).astype(BF16)


def fc1_call(normed, w, bias):
    tile = 256
    n = w.shape[1]
    rows = lambda m: pl.BlockSpec((tile, m), lambda i: (i, 0))
    fixed = lambda a, b: pl.BlockSpec((a, b), lambda i: (0, 0))
    return pl.pallas_call(
        fc1_kernel,
        grid=(ROWS // tile,),
        in_specs=[rows(D), fixed(D, n), fixed(1, n)],
        out_specs=[rows(n), rows(n)],
        out_shape=[jax.ShapeDtypeStruct((ROWS, n), BF16)] * 2,
        compiler_params=params(),
        cost_estimate=cost(2 * ROWS * D * n, 2 * (ROWS * D + D * n + 2 * ROWS * n), ROWS * n),
        name="fc1",
    )(normed, w, bias)


def hidden_grad_kernel(grad, w, slope, out, bias_grad):
    v = jnp.dot(grad[...], w[...], preferred_element_type=F32) * slope[...].astype(F32)
    low = v.astype(BF16)
    out[...] = low

    @pl.when(pl.program_id(0) == 0)
    def _():
        bias_grad[...] = jnp.zeros_like(bias_grad)

    bias_grad[...] += jnp.sum(low.astype(F32), axis=0, keepdims=True)


def hidden_grad_call(grad, w, slope):
    tile = 256
    n = w.shape[1]
    rows = lambda m: pl.BlockSpec((tile, m), lambda i: (i, 0))
    fixed = lambda a, b: pl.BlockSpec((a, b), lambda i: (0, 0))
    return pl.pallas_call(
        hidden_grad_kernel,
        grid=(ROWS // tile,),
        in_specs=[rows(D), fixed(D, n), rows(n)],
        out_specs=[rows(n), fixed(1, n)],
        out_shape=[jax.ShapeDtypeStruct((ROWS, n), BF16), jax.ShapeDtypeStruct((1, n), F32)],
        compiler_params=params(),
        cost_estimate=cost(2 * ROWS * D * n, 2 * (ROWS * D + D * n + 2 * ROWS * n)),
        name="hidden_grad",
    )(grad, w, slope)


def weight_grad_kernel(left, *refs):
    out = refs[-1]
    at = 0
    for right in refs[:-1]:
        n = right.shape[1]
        out[:, at : at + n] = jnp.dot(left[...], right[...], preferred_element_type=F32).astype(BF16)
        at += n


def weight_grad(left_t, right):
    n = right.shape[1]

    def block(i, m):
        return pl.pallas_call(
            weight_grad_kernel,
            grid=(m,),
            in_specs=[
                pl.BlockSpec((BLK, ROWS), lambda j: (i + j, 0)),
                pl.BlockSpec((ROWS, n), lambda j: (0, 0)),
            ],
            out_specs=pl.BlockSpec((BLK, n), lambda j: (j, 0)),
            out_shape=jax.ShapeDtypeStruct((m * BLK, n), BF16),
            compiler_params=params(),
            cost_estimate=cost(2 * m * BLK * ROWS * n, 2 * (m * BLK * ROWS + ROWS * n + m * BLK * n)),
            name="weight_grad",
        )(left_t, right)

    return block


def two_products_kernel(place, *refs):
    a, b, w1, w2, out = refs[0:4], refs[4:8], refs[8], refs[9], refs[10]
    nt = (((1,), (1,)), ((), ()))
    left = jnp.concatenate([r[...] for r in a], axis=0)
    right = jnp.concatenate([r[...] for r in b], axis=0)
    total = lax.dot_general(left, w1[...], nt, preferred_element_type=F32)
    total += lax.dot_general(right, w2[...], nt, preferred_element_type=F32)
    out[...] = total.astype(BF16)


def two_products(place, other, a, b, w1, col1, w2, col2):
    ka, kb = a.shape[1], b.shape[1]

    def rows(k, j):
        def at(i, p):
            core = 1 - p[3] if other else p[3]
            return core * 4 + lax.rem(p[4] + j, 4), 0

        return pl.BlockSpec((128, k), at)

    return pl.pallas_call(
        two_products_kernel,
        grid_spec=pltpu.PrefetchScalarGridSpec(
            num_scalar_prefetch=1,
            grid=(8,),
            in_specs=[rows(ka, j) for j in range(4)]
            + [rows(kb, j) for j in range(4)]
            + [
                pl.BlockSpec((BLK, ka), lambda i, p: (i, col1)),
                pl.BlockSpec((BLK, kb), lambda i, p: (i, col2)),
            ],
            out_specs=pl.BlockSpec((HALF, BLK), lambda i, p: (0, i)),
        ),
        out_shape=jax.ShapeDtypeStruct((HALF, D), BF16),
        compiler_params=params(),
        cost_estimate=cost(2 * HALF * D * (ka + kb), 2 * (HALF + D) * (ka + kb) + 2 * HALF * D),
        name="two_products",
    )(place, *([a] * 4), *([b] * 4), w1, w2)


def gain_kernel(place, a, b, *refs):
    units, gain, shift = refs[:8], refs[8], refs[9]
    unit = jnp.concatenate([r[...] for r in units], axis=0)
    v = jnp.concatenate([a[...], b[...]], axis=0).astype(F32)
    gain[...] = jnp.sum(v * unit.astype(F32), axis=0, keepdims=True)
    shift[...] = jnp.sum(v, axis=0, keepdims=True)


def gain_call(place, a, b, unit):
    def rows(other, j):
        def at(i, p):
            core = 1 - p[3] if other else p[3]
            return core * 4 + lax.rem(p[4] + j, 4), i

        return pl.BlockSpec((128, BLK), at)

    part = pl.BlockSpec((HALF, BLK), lambda i, p: (0, i))
    vec = pl.BlockSpec((1, BLK), lambda i, p: (0, i))
    return pl.pallas_call(
        gain_kernel,
        grid_spec=pltpu.PrefetchScalarGridSpec(
            num_scalar_prefetch=1,
            grid=(8,),
            in_specs=[part, part] + [rows(True, j) for j in range(4)] + [rows(False, j) for j in range(4)],
            out_specs=[vec, vec],
        ),
        out_shape=[jax.ShapeDtypeStruct((1, D), F32)] * 2,
        compiler_params=params(),
        cost_estimate=cost(3 * ROWS * D, 4 * ROWS * D),
        name="gain_grads",
    )(place, a, b, *([unit] * 8))


def forward_rows_kernel(place, p0, p1, p2, p3, tok, bias, out, full):
    y, x_lo = place[0], place[1]
    total = (p0[...].astype(F32) + p2[...].astype(F32)) + (p1[...].astype(F32) + p3[...].astype(F32))
    for j in range(8):
        full[:, pl.ds(pl.multiple_of(block_order(y, x_lo, j) * BLK, BLK), BLK)] = total[:, j * BLK : (j + 1) * BLK]
    out[...] = (tok[...].astype(F32) + full[...] + bias[...]).astype(BF16)


def backward_rows_kernel(place, p0, p1, p2, p3, tok, grad, gain, out, full):
    y, x_lo = place[0], place[1]
    total = (p0[...].astype(F32) + p2[...].astype(F32)) + (p1[...].astype(F32) + p3[...].astype(F32))
    for j in range(8):
        full[:, pl.ds(pl.multiple_of(block_order(y, x_lo, j) * BLK, BLK), BLK)] = total[:, j * BLK : (j + 1) * BLK]
    rows = tok[...].astype(F32)
    centered = rows - jnp.mean(rows, axis=-1, keepdims=True)
    inv = lax.rsqrt(jnp.mean(centered * centered, axis=-1, keepdims=True) + EPSILON)
    unit = centered * inv
    g = full[...] * gain[...]
    inner = g - jnp.mean(g, axis=-1, keepdims=True) - unit * jnp.mean(g * unit, axis=-1, keepdims=True)
    out[...] = (grad[...].astype(F32) + inv * inner).astype(BF16)


def finish_rows(kernel, place, parts, own_rows, vec, name):
    chunk = pl.BlockSpec((128, D), lambda i, p: (0, 0))
    mine = pl.BlockSpec((128, D), lambda i, p: (p[4], 0))
    fixed = pl.BlockSpec((1, D), lambda i, p: (0, 0))
    return pl.pallas_call(
        kernel,
        grid_spec=pltpu.PrefetchScalarGridSpec(
            num_scalar_prefetch=1,
            grid=(1,),
            in_specs=[chunk] * 4 + [mine] * len(own_rows) + [fixed],
            out_specs=chunk,
            scratch_shapes=[pltpu.VMEM((128, D), F32)],
        ),
        out_shape=jax.ShapeDtypeStruct((128, D), BF16),
        compiler_params=params(),
        cost_estimate=cost(20 * 128 * D, 14 * 128 * D),
        name=name,
    )(place, *parts, *own_rows, vec)


def sum_rows(mine, theirs):
    got = plane(theirs, flip=1)
    parts = [add_low(mine[128 * j : 128 * (j + 1)], got[128 * j : 128 * (j + 1)]) for j in range(4)]
    return parts[0], along_z(parts[1], 1), along_z(parts[2], 2), along_z(parts[3], 3)


def spread_rows(chunk, z):
    got = [chunk, along_z(chunk, -1), along_z(chunk, -2), along_z(chunk, -3)]
    out = jnp.zeros((HALF, D), BF16)
    for j in range(4):
        out = lax.dynamic_update_slice(out, got[j], (lax.rem(z + j, 4) * 128, 0))
    return out


def body(tokens, ln_gain, ln_shift, out_bias, w_qkv, b_qkv, w_out, w_fc1, b_fc1, w_fc2, out_grad):
    f, c, z = lax.axis_index("fsdp"), lax.axis_index("ctx"), lax.axis_index("tp")
    y, x_lo, x_hi, core = f // 2, f % 2, c // 2, c % 2
    place = jnp.stack([y, x_lo, x_hi, core, z]).astype(jnp.int32)
    tokens, out_grad = tokens[0], out_grad[0]

    def pair(mine):
        other = plane(mine, flip=1)
        first = core == 0
        return jnp.concatenate([jnp.where(first, mine, other), jnp.where(first, other, mine)], axis=0)

    pack = jnp.concatenate(
        [ln_gain, ln_shift, out_bias, b_qkv.reshape(-1), b_fc1.reshape(-1), jnp.zeros((64,), BF16)]
    ).reshape(10, 128)
    small = jnp.stack([pack, plane(pack, dy=-1), plane(pack, dy=2), plane(pack, dy=1)])
    small = jnp.concatenate([small, plane(small, dx=1)]).reshape(8, 1280)
    order = jnp.stack([block_order(y, x_lo, j) for j in range(8)])
    where_is = jnp.sum(
        jnp.where(order[None, :] == jnp.arange(8)[:, None], jnp.arange(8)[None, :], 0), axis=1
    )
    small = jnp.take(small, where_is, axis=0)
    gain = small[:, :256].reshape(1, D).astype(F32)
    shift = small[:, 256:512].reshape(1, D).astype(F32)
    bias = small[:, 512:768].reshape(1, D).astype(F32)
    qkv_bias = small[:, 768:960].reshape(8, 3, 8, 8).transpose(1, 2, 0, 3).astype(F32)
    qkv_bias = lax.dynamic_slice_in_dim(qkv_bias, core * 4, 4, axis=1).reshape(1, 3 * BLK)
    up_bias = small[:, 960:1216].reshape(8, 32, 8).transpose(1, 0, 2).astype(F32)
    up_bias = lax.dynamic_slice_in_dim(up_bias, core * 16, 16, axis=0).reshape(1, 1024)

    tok = pair(tokens)
    grad = pair(out_grad)
    qkv_shard = lax.dynamic_slice_in_dim(w_qkv, core * BLK, BLK, axis=2).reshape(BLK, 3 * BLK)
    proj_shard = lax.dynamic_slice_in_dim(w_out, core * BLK, BLK, axis=0).T
    up_shard = lax.dynamic_slice_in_dim(w_fc1, core * 1024, 1024, axis=1)
    down_shard = lax.dynamic_slice_in_dim(w_fc2, core * 1024, 1024, axis=0).T
    w_attn = gather_weight(jnp.concatenate([qkv_shard, proj_shard], axis=1))
    w_up = gather_weight(up_shard)
    w_down = gather_weight(down_shard)

    lane = jnp.arange(BLK, dtype=jnp.int32) % HD
    freq = jnp.where(lane < ROT, 10000.0 ** (-2.0 * (lane % (ROT // 2)).astype(F32) / ROT), 0.0)
    sign = jnp.where(lane < ROT // 2, -1.0, 1.0)

    def tables(first):
        angle = (first + jnp.arange(ROWS, dtype=jnp.int32)).astype(F32)[:, None] * freq[None, :]
        return jnp.cos(angle), jnp.sin(angle) * sign[None, :]

    cos_r, sin_r = tables(0)
    cos, sin = tables(x_hi * ROWS)

    normed, normed_t, unit, grad_rel, grad_t, bias_grad = prep(place, tok, grad, gain, shift)
    q, kv, do = qkv_call(normed, grad_rel, w_attn, qkv_bias, cos, sin)
    kvr = across(kv, True)

    active, slope = fc1_call(normed, w_up, up_bias)
    down_piece = reduce_x_first(weight_grad(grad_t, active))
    hidden_grad, up_bias_grad = hidden_grad_call(grad_rel, w_down, slope)
    up_piece = reduce_y_first(weight_grad(normed_t, hidden_grad))

    att, dq, dkv, dkvr = attention(place, q, kv, kvr, do, cos, sin, cos_r, sin_r)
    dkv = (dkv + across(dkvr, False).astype(F32)).astype(BF16)
    raw_grad = jnp.concatenate([dq, dkv], axis=1)

    normed_theirs = two_products(place, True, raw_grad, hidden_grad, w_attn, 0, w_up, 0)
    normed_mine = two_products(place, False, raw_grad, hidden_grad, w_attn, 0, w_up, 0)
    qkv_bias_grad = jnp.sum(raw_grad.astype(F32), axis=0)
    attn_piece = reduce_y_first(
        lambda i, m: jnp.concatenate([weight_grad(normed_t, raw_grad)(i, m), weight_grad(grad_t, att)(i, m)], axis=1)
    )

    branch_theirs = two_products(place, True, att, active, w_attn, 3, w_down, 0)
    branch_mine = two_products(place, False, att, active, w_attn, 3, w_down, 0)
    branch = sum_rows(branch_mine, branch_theirs)
    layer_out = spread_rows(finish_rows(forward_rows_kernel, place, branch, [tokens], bias, "forward_rows"), z)

    gain_part, shift_part = gain_call(place, normed_theirs, normed_mine, unit)
    normed_grad = sum_rows(normed_mine, normed_theirs)
    input_grad = spread_rows(
        finish_rows(backward_rows_kernel, place, normed_grad, [tokens, out_grad], gain, "backward_rows"), z
    )

    def ring_sum(own, one, two, three):
        return (own + two) + (one + three)

    ln_vec = jnp.concatenate([gain_part, shift_part], axis=0)
    ln_vec = ring_sum(ln_vec, along_z(ln_vec, 1), along_z(ln_vec, 2), along_z(ln_vec, 3))
    ln_vec = ln_vec + plane(ln_vec, flip=1)
    by_block = jnp.concatenate([ln_vec, bias_grad], axis=0).reshape(3, 2, 4, BLK)
    units = jnp.concatenate([qkv_bias_grad, up_bias_grad.reshape(-1)])

    def message(dy):
        return jnp.concatenate([by_block[:, :, dy].reshape(-1), units])

    vec = ring_sum(message(0), plane(message(1), dy=1), plane(message(2), dy=2), plane(message(3), dy=3))
    at_x, units = vec[: 6 * BLK].reshape(3, 2, BLK), vec[6 * BLK :]
    to_side = jnp.concatenate([at_x[:, 1].reshape(-1), units])
    to_same = jnp.concatenate([at_x[:, 0].reshape(-1), units])
    vec = ring_sum(to_same, plane(to_side, dx=1), plane(to_same, dx=2), plane(to_side, dx=3))
    gain_grad, shift_grad, out_bias_grad = vec[:BLK], vec[BLK : 2 * BLK], vec[2 * BLK : 3 * BLK]
    units = vec[3 * BLK :]
    mine_first = core == 0

    def both(mine, axis):
        other = plane(mine, flip=1)
        return jnp.concatenate(
            [jnp.where(mine_first, mine, other), jnp.where(mine_first, other, mine)], axis=axis
        )

    units = both(units.reshape(1, 1792), 0)
    qkv_bias_out = lax.dynamic_slice_in_dim(
        units[:, : 3 * BLK].reshape(2, 3, 4, HD).transpose(1, 0, 2, 3).reshape(3, 8, HD), f * 8, 8, axis=2
    )
    up_bias_out = lax.dynamic_slice_in_dim(units[:, 3 * BLK :].reshape(32, HD), f * 8, 8, axis=1)

    attn_all = both(attn_piece[None], 0)
    qkv_out = attn_all[:, :, : 3 * BLK].reshape(2, BLK, 3, BLK).transpose(1, 2, 0, 3).reshape(BLK, 3, HALF)
    proj_out = attn_all[:, :, 3 * BLK :].transpose(0, 2, 1).reshape(HALF, BLK)
    up_out = both(up_piece, 1)
    down_out = both(down_piece, 1).T
    return (
        layer_out[None],
        input_grad[None],
        gain_grad,
        shift_grad,
        out_bias_grad,
        qkv_out.astype(F32),
        qkv_bias_out,
        proj_out.astype(F32),
        up_out.astype(F32),
        up_bias_out,
        down_out.astype(F32),
    )


def solution(mesh):
    in_specs = (
        P("fsdp", "ctx", None),
        P("fsdp"),
        P("fsdp"),
        P("fsdp"),
        P("fsdp", None, "tp"),
        P(None, "tp", "fsdp"),
        P("tp", "fsdp"),
        P("fsdp", "tp"),
        P("tp", "fsdp"),
        P("tp", "fsdp"),
        P("fsdp", "ctx", None),
    )
    out_specs = (
        P("fsdp", "ctx", None),
        P("fsdp", "ctx", None),
        P("fsdp"),
        P("fsdp"),
        P("fsdp"),
        P("fsdp", None, "tp"),
        P(None, "tp", "fsdp"),
        P("tp", "fsdp"),
        P("fsdp", "tp"),
        P("tp", "fsdp"),
        P("tp", "fsdp"),
    )
    return jax.shard_map(body, mesh=mesh, in_specs=in_specs, out_specs=out_specs, check_vma=False)
```

time: 1440 us -> 672 us (0.47)
  waiting for transfers between devices: 873 us -> 197 us
  blocking collectives: 267 us -> 0 us
  Pallas kernels: 0 us -> 214 us
  matrix products: 184 us -> 0 us
  starting transfers between devices: 1.46 us -> 144 us
  local copies, waits for them, and re-layouts: 23.9 us -> 58.1 us
  other arithmetic: 69.3 us -> 45.3 us
  between operations: 16.9 us -> 2.02 us
    all_gather x8 -> x0, waiting for transfers between devices: 399 us -> none  [the longest x1 161 us: body(): lax.all_gather(w_fc2, 'fsdp', axis=1, tiled=True)]
    reduce_scatter x6 -> x0, waiting for transfers between devices: 386 us -> none  [the longest x1 125 us: body(): lax.psum_scatter(up_grad.astype(jnp.bfloat16), ('fsdp', 'ctx'), scatter_d...]
    pallas_call x0 -> x42, Pallas kernels: none -> 214 us  [the longest x30 88.4 us: block(): pl.pallas_call(weight_grad_kernel, grid=(m,), in_specs=[pl.BlockSpec((BLK...]
    ppermute x0 -> x81, waiting for transfers between devices: none -> 197 us  [the longest x64 138 us: plane(): return lax.ppermute(arr, ('fsdp', 'ctx'), pairs)]
    dot_general x18 -> x0, matrix products: 184 us -> none  [the longest x1 23 us: body(): jnp.einsum('qhd,khd->hqk', grad_heads, values_full, preferred_element_typ...]
    ppermute x0 -> x81, starting transfers between devices: none -> 144 us  [the longest x64 117 us: plane(): return lax.ppermute(arr, ('fsdp', 'ctx'), pairs)]
    unnamed x2 -> x0, blocking collectives: 135 us -> none
    all_gather x9 -> x0, blocking collectives: 132 us -> none  [the longest x1 23.4 us: body(): lax.all_gather(b_qkv, 'fsdp', axis=2, tiled=True)]
  transfers between devices with their start and end apart: 15 -> 81, of which waited for: 13 -> 28; matrix products, arithmetic and copies ran while one was open for 19% -> 13% of each run, Pallas kernels for 0% -> 26%
where the time goes in v1:
time: 672 us; the launch traced here: 660 us
  Pallas kernels  214 us (32%)
  waiting for transfers between devices  197 us (29%)
  starting transfers between devices  144 us (21%)
  local copies, waits for them, and re-layouts  58.1 us (9%)
  other arithmetic  45.3 us (7%)
    ppermute x64, waiting for transfers between devices, plane(): return lax.ppermute(arr, ('fsdp', 'ctx'), pairs)  138 us
    ppermute x64, starting transfers between devices, plane(): return lax.ppermute(arr, ('fsdp', 'ctx'), pairs)  117 us
    pallas_call x30, Pallas kernels, block(): pl.pallas_call(weight_grad_kernel, grid=(m,), in_specs=[pl.BlockSpec((BLK...  88.4 us
    ppermute x15, waiting for transfers between devices, along_z(): return lax.ppermute(arr, 'tp', [(i, (i + dz) % 4) for i in range(4)])  58.7 us
    pallas_call x4, Pallas kernels, two_products(): pl.pallas_call(two_products_kernel, grid_spec=pltpu.PrefetchScalarGridSpe...  40.4 us
    unnamed x143, local copies, waits for them, and re-layouts  31.7 us
    pallas_call x1, Pallas kernels, attention(): pl.pallas_call(attention_kernel, grid_spec=pltpu.PrefetchScalarGridSpec(n...  25.9 us
    ppermute x15, starting transfers between devices, along_z(): return lax.ppermute(arr, 'tp', [(i, (i + dz) % 4) for i in range(4)])  22.6 us
  transfers between devices with their start and end apart: 81, of which 28 were waited for; matrix products, arithmetic and copies ran while one was open for 13% of the time, Pallas kernels for 26%

profile of v1, /device:TPU:1, one launch (start us, length us, event | category | flops | bytes accessed | tf_op | source)
XLA Modules:
  0.0 660.1 jit_solution(4155638325143302227)
XLA Ops:
  4.5 3.6 collective-permute-start.2
  17.4 8.9 %fusion.1 = (f32[1024,256]{1,0:T(8,128)}, f32[1024,256]{1,0:T(8,128)}, f32[1024,256]{1,0:T(8,128)}, f32[1024,256]{1,0:T(8,128)}) fusion(f32[1024]{0:T(1024)S(1)} %get-tuple-element.151, f32[256]{0:T(256)S(1)} %get-tuple-element.147, f32[256]{0:T(256)S(1)} %get-tuple-element.148, f32[1024]{0:T(1024)S(1)} %get-tuple-element.152), kind=kLoop, calls=%fused_computation.16 | loop fusion | flops 1048576 | bytes 4204544 | tf_op jit(solution)/shard_map/mul | solution.py:606
  30.8 10.0 %collective-permute-done.5 = bf16[4,10,128]{2,1,0:T(8,128)(2,1)S(1)} collective-permute-done((bf16[4,10,128]{2,1,0:T(8,128)(2,1)S(1)}, bf16[4,10,128]{2,1,0:T(8,128)(2,1)S(1)}, u32[]{:S(2)}, u32[]{:S(2)}) %collective-permute-start.5) | collective-permute-done | bytes 10272 | tf_op jit(solution)/shard_map/ppermute | solution.py:43
  47.4 4.5 collective-permute-done.14
  55.7 8.6 %collective-permute-start.23 = (bf16[256,1024]{1,0:T(8,128)(2,1)S(1)}, bf16[256,1024]{1,0:T(8,128)(2,1)}, u32[]{:S(2)}, u32[]{:S(2)}) collective-permute-start(bf16[256,1024]{1,0:T(8,128)(2,1)S(1)} %bitcast.117), channel_id=1, source_target_pairs={{0,32},{4,36},{8,40},{12,44},{16,48},{20,52},{24,56},{28,60},{32,6... | collective-permute-start | bytes 1572872 | tf_op jit(solution)/shard_map/ppermute | solution.py:43
  67.6 6.9 %collective-permute-done.16 = bf16[256,1024]{1,0:T(8,128)(2,1)S(1)} collective-permute-done((bf16[256,1024]{1,0:T(8,128)(2,1)}, bf16[256,1024]{1,0:T(8,128)(2,1)S(1)}, u32[]{:S(2)}, u32[]{:S(2)}) %collective-permute-start.16) | collective-permute-done | bytes 524320 | tf_op jit(solution)/shard_map/ppermute | solution.py:43
  83.4 5.8 collective-permute-start.1
  89.3 3.8 collective-permute-done.23
  100.4 5.8 collective-permute-done.11
  109.7 7.7 %collective-permute-done.12 = bf16[256,1024]{1,0:T(8,128)(2,1)S(1)} collective-permute-done((bf16[256,1024]{1,0:T(8,128)(2,1)}, bf16[256,1024]{1,0:T(8,128)(2,1)S(1)}, u32[]{:S(2)}, u32[]{:S(2)}) %collective-permute-start.12) | collective-permute-done | bytes 524320 | tf_op jit(solution)/shard_map/ppermute | solution.py:43
  122.9 5.7 collective-permute-done.19
  132.0 7.9 %collective-permute-done.20 = bf16[256,1024]{1,0:T(8,128)(2,1)S(1)} collective-permute-done((bf16[256,1024]{1,0:T(8,128)(2,1)S(1)}, bf16[256,1024]{1,0:T(8,128)(2,1)S(1)}, u32[]{:S(2)}, u32[]{:S(2)}) %collective-permute-start.20) | collective-permute-done | bytes 524320 | tf_op jit(solution)/shard_map/ppermute | solution.py:43
  142.6 8.6 %collective-permute-done.26 = bf16[256,1024]{1,0:T(8,128)(2,1)S(1)} collective-permute-done((bf16[256,1024]{1,0:T(8,128)(2,1)}, bf16[256,1024]{1,0:T(8,128)(2,1)S(1)}, u32[]{:S(2)}, u32[]{:S(2)}) %collective-permute-start.26) | collective-permute-done | bytes 524320 | tf_op jit(solution)/shard_map/ppermute | solution.py:43
  151.2 11.2 %collective-permute-done.27 = bf16[256,1024]{1,0:T(8,128)(2,1)S(1)} collective-permute-done((bf16[256,1024]{1,0:T(8,128)(2,1)}, bf16[256,1024]{1,0:T(8,128)(2,1)S(1)}, u32[]{:S(2)}, u32[]{:S(2)}) %collective-permute-start.27) | collective-permute-done | bytes 524320 | tf_op jit(solution)/shard_map/ppermute | solution.py:43
  169.5 12.8 %prep.1 = (bf16[1024,2048]{1,0:T(8,128)(2,1)}, bf16[2048,1024]{1,0:T(8,128)(2,1)}, bf16[1024,2048]{1,0:T(8,128)(2,1)}, bf16[1024,2048]{1,0:T(8,128)(2,1)}, bf16[...) custom-call(s32[5]{0:T(128)} %stack.62.place, bf16[1024,2048]{1,0:T(8,128)(2,1)} %pad_maximum_fusion.tok, ...), custom_call_target="tpu_custom_call" | custom-call | flops 83886080 | bytes 29360128 | tf_op jit(solution)/shard_map/prep/pallas_call | solution.py:135
  182.3 11.0 %fc1.1 = (bf16[1024,1024]{1,0:T(8,128)(2,1)}, bf16[1024,1024]{1,0:T(8,128)(2,1)}) custom-call(bf16[1024,2048]{1,0:T(8,128)(2,1)} %get-tuple-element.30.normed, bf16[2048,1024]{1,0:T(8,128)(2,1)} %copy-done.5, f32[1,1024]{1,0:T(1,128)} %reshape.209.bias), custom_call_target="tpu_custom_call" | custom-call | flops 4294967296 | bytes 12582912 | tf_op jit(solution)/shard_map/fc1/pallas_call | solution.py:361
  193.3 8.9 %hidden_grad.1 = (bf16[1024,1024]{1,0:T(8,128)(2,1)}, f32[1,1024]{1,0:T(1,128)}) custom-call(bf16[1024,2048]{1,0:T(8,128)(2,1)} %get-tuple-element.31.grad, bf16[2048,1024]{1,0:T(8,128)(2,1)} %copy-done.3, bf16[1024,1024]{1,0:T(8,128)(2,1)} %get-tuple-element.40.slope), custom_call_target="tpu_custom_call" | custom-call | flops 4294967296 | bytes 12582912 | tf_op jit(solution)/shard_map/hidden_grad/pallas_call | solution.py:390
  208.8 3.4 weight_grad.51
  214.0 10.2 %qkv.1 = (bf16[1024,256]{1,0:T(8,128)(2,1)}, bf16[1024,512]{1,0:T(8,128)(2,1)}, bf16[1024,256]{1,0:T(8,128)(2,1)}) custom-call(bf16[1024,2048]{1,0:T(8,128)(2,1)} %get-tuple-element.30.normed, bf16[1024,2048]{1,0:T(8,128)(2,1)} %get-tuple-element.31.grad, bf16[2048,1024]{1,0:T(8,128)(2,1)} %constant_dynamic-update-slice_fusion.w.refs_8_, ...), custom_call_target="tpu_custom_call" | custom-call | flops 4294967296 | bytes 33554432 | tf_op jit(solution)/shard_map/qkv/pallas_call | solution.py:179
  224.1 3.5 collective-permute-start.13
  237.2 3.3 weight_grad.47
  243.8 3.3 weight_grad.50
  250.4 3.4 weight_grad.59
  263.9 4.0 weight_grad.58
  267.9 4.1 weight_grad.55
  276.8 25.9 %attention.1 = (bf16[1024,256]{1,0:T(8,128)(2,1)}, bf16[1024,256]{1,0:T(8,128)(2,1)}, f32[1024,512]{1,0:T(8,128)}, bf16[1024,512]{1,0:T(8,128)(2,1)}) custom-call(s32[5]{0:T(128)} %stack.62.place, bf16[1024,256]{1,0:T(8,128)(2,1)} %get-tuple-element.32.q, bf16[1024,512]{1,0:T(8,128)(2,1)} %get-tuple-element.33.kv, bf16[1024,512]{1,0:T(8,128)(2,1)} %copy-done.53, ...), custom_call_target="tpu_custom_call" | custom-call | flops 19327352832 | bytes 12582912 | tf_op jit(solution)/shard_map/attention/pallas_call | solution.py:308
  302.7 9.6 %two_products.5 = bf16[512,2048]{1,0:T(8,128)(2,1)} custom-call(s32[5]{0:T(128)} %stack.62.place, bf16[1024,256]{1,0:T(8,128)(2,1)} %get-tuple-element.35.refs_0_.refs_1_.refs_2_.refs_3_, bf16[1024,256]{1,0:T(8,128)(2,1)} %get-tuple-element.35.refs_0_.refs_1_.refs_2_.refs_3_, bf16[1024,256]{1,0:T(8,128)(2,1)} %get-tuple-element.35.refs_0_.refs_1_.refs_2_.refs_3_, ...), custom_call_target="tpu_custom_call" | custom-call | flops 2684354560 | bytes 8650752 | tf_op jit(solution)/shard_map/two_products/pallas_call | solution.py:452
  312.3 4.5 collective-permute-start.28
  338.6 9.5 %two_products.4 = bf16[512,2048]{1,0:T(8,128)(2,1)} custom-call(s32[5]{0:T(128)} %stack.62.place, bf16[1024,256]{1,0:T(8,128)(2,1)} %get-tuple-element.35.refs_0_.refs_1_.refs_2_.refs_3_, bf16[1024,256]{1,0:T(8,128)(2,1)} %get-tuple-element.35.refs_0_.refs_1_.refs_2_.refs_3_, bf16[1024,256]{1,0:T(8,128)(2,1)} %get-tuple-element.35.refs_0_.refs_1_.refs_2_.refs_3_, ...), custom_call_target="tpu_custom_call" | custom-call | flops 2684354560 | bytes 8650752 | tf_op jit(solution)/shard_map/two_products/pallas_call | solution.py:452
  350.9 24.3 %collective-permute-start.79 = (bf16[256,1024]{1,0:T(8,128)(2,1)S(1)}, bf16[256,1024]{1,0:T(8,128)(2,1)S(1)}, u32[]{:S(2)}, u32[]{:S(2)}) collective-permute-start(bf16[256,1024]{1,0:T(8,128)(2,1)S(1)} %add_convert_fusion.2), channel_id=1, source_target_pairs={{0,8},{4,12},{8,0},{12,4},{16,24},{20,28},{24,16},{28,20},{32,40},... | collective-permute-start | bytes 1572872 | tf_op jit(solution)/shard_map/ppermute | solution.py:43
  376.9 31.5 %collective-permute-done.79 = bf16[256,1024]{1,0:T(8,128)(2,1)S(1)} collective-permute-done((bf16[256,1024]{1,0:T(8,128)(2,1)S(1)}, bf16[256,1024]{1,0:T(8,128)(2,1)S(1)}, u32[]{:S(2)}, u32[]{:S(2)}) %collective-permute-start.79) | collective-permute-done | bytes 524320 | tf_op jit(solution)/shard_map/ppermute | solution.py:43
  412.1 10.7 %two_products.7.a = bf16[512,2048]{1,0:T(8,128)(2,1)} custom-call(s32[5]{0:T(128)} %stack.62.place, bf16[1024,768]{1,0:T(8,128)(2,1)} %pad_maximum_fusion.2.refs_0_.refs_1_.refs_2_.refs_3_, bf16[1024,768]{1,0:T(8,128)(2,1)} %pad_maximum_fusion.2.refs_0_.refs_1_.refs_2_.refs_3_, bf16[1024,768]{1,0:T(8,128)(2,1)} %pad_maximum_fusion.2.refs_0_.refs_1_.refs_2_.refs_3_, ...), custom_call_target="tpu_custom_call" | custom-call | flops 3758096384 | bytes 11272192 | tf_op jit(solution)/shard_map/two_products/pallas_call | solution.py:452
  422.8 10.7 %two_products.6.b = bf16[512,2048]{1,0:T(8,128)(2,1)} custom-call(s32[5]{0:T(128)} %stack.62.place, bf16[1024,768]{1,0:T(8,128)(2,1)} %pad_maximum_fusion.2.refs_0_.refs_1_.refs_2_.refs_3_, bf16[1024,768]{1,0:T(8,128)(2,1)} %pad_maximum_fusion.2.refs_0_.refs_1_.refs_2_.refs_3_, bf16[1024,768]{1,0:T(8,128)(2,1)} %pad_maximum_fusion.2.refs_0_.refs_1_.refs_2_.refs_3_, ...), custom_call_target="tpu_custom_call" | custom-call | flops 3758096384 | bytes 11272192 | tf_op jit(solution)/shard_map/two_products/pallas_call | solution.py:452
  433.4 7.7 %gain_grads.1 = (f32[1,2048]{1,0:T(1,128)}, f32[1,2048]{1,0:T(1,128)}) custom-call(s32[5]{0:T(128)} %stack.62.place, bf16[512,2048]{1,0:T(8,128)(2,1)} %two_products.7.a, bf16[512,2048]{1,0:T(8,128)(2,1)} %two_products.6.b, bf16[1024,2048]{1,0:T(8,128)(2,1)} %get-tuple-element.42.refs_0_.refs_1_.refs_2_.refs_3_.refs_4_.refs_5_.refs_6_.refs_7_, ...), custom_call_target="tpu_custom_call" | custom-call | flops 6291456 | bytes 8388608 | tf_op jit(solution)/shard_map/gain_grads/pallas_call | solution.py:490
  502.9 10.9 %collective-permute-done.57 = bf16[256,1024]{1,0:T(8,128)(2,1)S(1)} collective-permute-done((bf16[256,1024]{1,0:T(8,128)(2,1)}, bf16[256,1024]{1,0:T(8,128)(2,1)S(1)}, u32[]{:S(2)}, u32[]{:S(2)}) %collective-permute-start.57) | collective-permute-done | bytes 524320 | tf_op jit(solution)/shard_map/ppermute | solution.py:43
  513.8 3.9 collective-permute-start.54
  524.4 9.5 %collective-permute-done.54 = bf16[256,1024]{1,0:T(8,128)(2,1)S(1)} collective-permute-done((bf16[256,1024]{1,0:T(8,128)(2,1)}, bf16[256,1024]{1,0:T(8,128)(2,1)S(1)}, u32[]{:S(2)}, u32[]{:S(2)}) %collective-permute-start.54) | collective-permute-done | bytes 524320 | tf_op jit(solution)/shard_map/ppermute | solution.py:43
  545.2 7.1 %collective-permute-done.61 = bf16[256,1024]{1,0:T(8,128)(2,1)S(1)} collective-permute-done((bf16[256,1024]{1,0:T(8,128)(2,1)S(1)}, bf16[256,1024]{1,0:T(8,128)(2,1)S(1)}, u32[]{:S(2)}, u32[]{:S(2)}) %collective-permute-start.61) | collective-permute-done | bytes 524320 | tf_op jit(solution)/shard_map/ppermute | solution.py:43
  556.5 9.1 %collective-permute-done.30.p2 = bf16[128,2048]{1,0:T(8,128)(2,1)} collective-permute-done((bf16[128,2048]{1,0:T(8,128)(2,1)}, bf16[128,2048]{1,0:T(8,128)(2,1)}, u32[]{:S(2)}, u32[]{:S(2)}) %collective-permute-start.30) | collective-permute-done | bytes 524320 | tf_op jit(solution)/shard_map/ppermute | solution.py:56
  567.8 4.0 forward_rows.1
  571.8 3.4 collective-permute-start.32
  596.0 12.7 %collective-permute-done.32 = bf16[128,2048]{1,0:T(8,128)(2,1)} collective-permute-done((bf16[128,2048]{1,0:T(8,128)(2,1)}, bf16[128,2048]{1,0:T(8,128)(2,1)}, u32[]{:S(2)}, u32[]{:S(2)}) %collective-permute-start.32) | collective-permute-done | bytes 524320 | tf_op jit(solution)/shard_map/ppermute | solution.py:56
  608.7 3.6 collective-permute-start.39
  614.5 8.9 %collective-permute-done.38.p2 = bf16[128,2048]{1,0:T(8,128)(2,1)S(1)} collective-permute-done((bf16[128,2048]{1,0:T(8,128)(2,1)S(1)}, bf16[128,2048]{1,0:T(8,128)(2,1)S(1)}, u32[]{:S(2)}, u32[]{:S(2)}) %collective-permute-start.38) | collective-permute-done | bytes 524320 | tf_op jit(solution)/shard_map/ppermute | solution.py:56
  624.4 4.5 backward_rows.1
  633.1 7.8 %collective-permute-done.40 = bf16[128,2048]{1,0:T(8,128)(2,1)S(1)} collective-permute-done((bf16[128,2048]{1,0:T(8,128)(2,1)}, bf16[128,2048]{1,0:T(8,128)(2,1)S(1)}, u32[]{:S(2)}, u32[]{:S(2)}) %collective-permute-start.40) | collective-permute-done | bytes 524320 | tf_op jit(solution)/shard_map/ppermute | solution.py:56
  640.9 3.9 collective-permute-done.41
  644.9 13.6 %collective-permute-done.42 = bf16[128,2048]{1,0:T(8,128)(2,1)S(1)} collective-permute-done((bf16[128,2048]{1,0:T(8,128)(2,1)}, bf16[128,2048]{1,0:T(8,128)(2,1)S(1)}, u32[]{:S(2)}, u32[]{:S(2)}) %collective-permute-start.42) | collective-permute-done | bytes 524320 | tf_op jit(solution)/shard_map/ppermute | solution.py:56
  (411 shorter events, 253.8 us)
Async XLA Ops:
  4.5 23.0 %collective-permute-start.2 = (bf16[10,128]{1,0:T(8,128)(2,1)S(1)}, bf16[10,128]{1,0:T(8,128)(2,1)S(1)}, u32[]{:S(2)}, u32[]{:S(2)}) collective-permute-start(bf16[10,128]{1,0:T(8,128)(2,1)S(1)} %bitcast.128), channel_id=1, source_target_pairs={{0,96},{4,100},{8,104},{12,108},{16,112},{20,116},{24,120},{28,124... | collective-permute-start | bytes 7688 | tf_op jit(solution)/shard_map/ppermute | solution.py:43
  12.6 31.2 %collective-permute-start.6 = (bf16[256,1024]{1,0:T(8,128)(2,1)}, bf16[256,1024]{1,0:T(8,128)(2,1)}, u32[]{:S(2)}, u32[]{:S(2)}) collective-permute-start(bf16[256,1024]{1,0:T(8,128)(2,1)} %get-tuple-element.125), channel_id=1, source_target_pairs={{0,96},{4,100},{8,104},{12,108},{16,112},{20,116},{24,120},{28,124... | collective-permute-start | bytes 1572872 | tf_op jit(solution)/shard_map/ppermute | solution.py:43
  14.6 29.6 %collective-permute-start.7 = (bf16[256,1024]{1,0:T(8,128)(2,1)}, bf16[256,1024]{1,0:T(8,128)(2,1)}, u32[]{:S(2)}, u32[]{:S(2)}) collective-permute-start(bf16[256,1024]{1,0:T(8,128)(2,1)} %get-tuple-element.125), channel_id=1, source_target_pairs={{0,64},{4,68},{8,72},{12,76},{16,80},{20,84},{24,88},{28,92},{32,9... | collective-permute-start | bytes 1572872 | tf_op jit(solution)/shard_map/ppermute | solution.py:43
  44.2 30.2 %collective-permute-start.16 = (bf16[256,1024]{1,0:T(8,128)(2,1)}, bf16[256,1024]{1,0:T(8,128)(2,1)S(1)}, u32[]{:S(2)}, u32[]{:S(2)}) collective-permute-start(bf16[256,1024]{1,0:T(8,128)(2,1)} %get-tuple-element.100), channel_id=1, source_target_pairs={{0,32},{4,36},{8,40},{12,44},{16,48},{20,52},{24,56},{28,60},{32,6... | collective-permute-start | bytes 1572872 | tf_op jit(solution)/shard_map/ppermute | solution.py:43
  44.6 35.6 %collective-permute-start.17 = (bf16[256,1024]{1,0:T(8,128)(2,1)}, bf16[256,1024]{1,0:T(8,128)(2,1)}, u32[]{:S(2)}, u32[]{:S(2)}) collective-permute-start(bf16[256,1024]{1,0:T(8,128)(2,1)} %get-tuple-element.100), channel_id=1, source_target_pairs={{0,16},{4,20},{8,24},{12,28},{16,8},{20,12},{24,0},{28,4},{32,48},... | collective-permute-start | bytes 1572872 | tf_op jit(solution)/shard_map/ppermute | solution.py:43
  44.8 38.5 %collective-permute-start.21 = (bf16[256,1024]{1,0:T(8,128)(2,1)S(1)}, bf16[256,1024]{1,0:T(8,128)(2,1)}, u32[]{:S(2)}, u32[]{:S(2)}) collective-permute-start(bf16[256,1024]{1,0:T(8,128)(2,1)S(1)} %bitcast.115), channel_id=1, source_target_pairs={{0,96},{4,100},{8,104},{12,108},{16,112},{20,116},{24,120},{28,124... | collective-permute-start | bytes 1572872 | tf_op jit(solution)/shard_map/ppermute | solution.py:43
  51.8 37.4 %collective-permute-start.22 = (bf16[256,1024]{1,0:T(8,128)(2,1)S(1)}, bf16[256,1024]{1,0:T(8,128)(2,1)}, u32[]{:S(2)}, u32[]{:S(2)}) collective-permute-start(bf16[256,1024]{1,0:T(8,128)(2,1)S(1)} %bitcast.116), channel_id=1, source_target_pairs={{0,64},{4,68},{8,72},{12,76},{16,80},{20,84},{24,88},{28,92},{32,9... | collective-permute-start | bytes 1572872 | tf_op jit(solution)/shard_map/ppermute | solution.py:43
  55.7 37.4 %collective-permute-start.23 = (bf16[256,1024]{1,0:T(8,128)(2,1)S(1)}, bf16[256,1024]{1,0:T(8,128)(2,1)}, u32[]{:S(2)}, u32[]{:S(2)}) collective-permute-start(bf16[256,1024]{1,0:T(8,128)(2,1)S(1)} %bitcast.117), channel_id=1, source_target_pairs={{0,32},{4,36},{8,40},{12,44},{16,48},{20,52},{24,56},{28,60},{32,6... | collective-permute-start | bytes 1572872 | tf_op jit(solution)/shard_map/ppermute | solution.py:43
  83.4 79.0 %collective-permute-start.1 = (bf16[512,2048]{1,0:T(8,128)(2,1)}, bf16[512,2048]{1,0:T(8,128)(2,1)S(1)}, u32[]{:S(2)}, u32[]{:S(2)}) collective-permute-start(bf16[512,2048]{1,0:T(8,128)(2,1)} %bitcast.111), channel_id=1, source_target_pairs={{0,4},{4,0},{8,12},{12,8},{16,20},{20,16},{24,28},{28,24},{32,36},... | collective-permute-start | bytes 6291464 | tf_op jit(solution)/shard_map/ppermute | solution.py:43
  89.2 73.2 %collective-permute-start = (bf16[512,2048]{1,0:T(8,128)(2,1)S(1)}, bf16[512,2048]{1,0:T(8,128)(2,1)S(1)}, u32[]{:S(2)}, u32[]{:S(2)}) collective-permute-start(bf16[512,2048]{1,0:T(8,128)(2,1)S(1)} %bitcast.110), channel_id=1, source_target_pairs={{0,4},{4,0},{8,12},{12,8},{16,20},{20,16},{24,28},{28,24},{32,36},... | collective-permute-start | bytes 6291464 | tf_op jit(solution)/shard_map/ppermute | solution.py:43
  95.5 22.0 %collective-permute-start.12 = (bf16[256,1024]{1,0:T(8,128)(2,1)}, bf16[256,1024]{1,0:T(8,128)(2,1)S(1)}, u32[]{:S(2)}, u32[]{:S(2)}) collective-permute-start(bf16[256,1024]{1,0:T(8,128)(2,1)} %collective-permute-done.8), channel_id=1, source_target_pairs={{0,24},{4,28},{8,16},{12,20},{16,0},{20,4},{24,8},{28,12},{32,56},... | collective-permute-start | bytes 1572872 | tf_op jit(solution)/shard_map/ppermute | solution.py:43
  98.3 23.8 %collective-permute-start.18 = (bf16[256,1024]{1,0:T(8,128)(2,1)}, bf16[256,1024]{1,0:T(8,128)(2,1)S(1)}, u32[]{:S(2)}, u32[]{:S(2)}) collective-permute-start(bf16[256,1024]{1,0:T(8,128)(2,1)} %collective-permute-done.14), channel_id=1, source_target_pairs={{0,16},{4,20},{8,24},{12,28},{16,8},{20,12},{24,0},{28,4},{32,48},... | collective-permute-start | bytes 1572872 | tf_op jit(solution)/shard_map/ppermute | solution.py:43
  106.2 22.5 %collective-permute-start.19 = (bf16[256,1024]{1,0:T(8,128)(2,1)}, bf16[256,1024]{1,0:T(8,128)(2,1)S(1)}, u32[]{:S(2)}, u32[]{:S(2)}) collective-permute-start(bf16[256,1024]{1,0:T(8,128)(2,1)} %collective-permute-done.15), channel_id=1, source_target_pairs={{0,24},{4,28},{8,16},{12,20},{16,0},{20,4},{24,8},{28,12},{32,56},... | collective-permute-start | bytes 1572872 | tf_op jit(solution)/shard_map/ppermute | solution.py:43
  117.4 22.5 %collective-permute-start.20 = (bf16[256,1024]{1,0:T(8,128)(2,1)S(1)}, bf16[256,1024]{1,0:T(8,128)(2,1)S(1)}, u32[]{:S(2)}, u32[]{:S(2)}) collective-permute-start(bf16[256,1024]{1,0:T(8,128)(2,1)S(1)} %collective-permute-done.16), channel_id=1, source_target_pairs={{0,24},{4,28},{8,16},{12,20},{16,0},{20,4},{24,8},{28,12},{32,56},... | collective-permute-start | bytes 1572872 | tf_op jit(solution)/shard_map/ppermute | solution.py:43
  128.7 22.5 %collective-permute-start.26 = (bf16[256,1024]{1,0:T(8,128)(2,1)}, bf16[256,1024]{1,0:T(8,128)(2,1)S(1)}, u32[]{:S(2)}, u32[]{:S(2)}) collective-permute-start(bf16[256,1024]{1,0:T(8,128)(2,1)} %collective-permute-done.22), channel_id=1, source_target_pairs={{0,24},{4,28},{8,16},{12,20},{16,0},{20,4},{24,8},{28,12},{32,56},... | collective-permute-start | bytes 1572872 | tf_op jit(solution)/shard_map/ppermute | solution.py:43
  139.9 22.5 %collective-permute-start.27 = (bf16[256,1024]{1,0:T(8,128)(2,1)}, bf16[256,1024]{1,0:T(8,128)(2,1)S(1)}, u32[]{:S(2)}, u32[]{:S(2)}) collective-permute-start(bf16[256,1024]{1,0:T(8,128)(2,1)} %collective-permute-done.23), channel_id=1, source_target_pairs={{0,24},{4,28},{8,16},{12,20},{16,0},{20,4},{24,8},{28,12},{32,56},... | collective-permute-start | bytes 1572872 | tf_op jit(solution)/shard_map/ppermute | solution.py:43
  212.1 41.6 %collective-permute-start.69 = (bf16[256,1024]{1,0:T(8,128)(2,1)S(1)}, bf16[256,1024]{1,0:T(8,128)(2,1)S(1)}, u32[]{:S(2)}, u32[]{:S(2)}) collective-permute-start(bf16[256,1024]{1,0:T(8,128)(2,1)S(1)} %copy-done.44), channel_id=1, source_target_pairs={{0,64},{4,68},{8,72},{12,76},{16,80},{20,84},{24,88},{28,92},{32,9... | collective-permute-start | bytes 1572872 | tf_op jit(solution)/shard_map/ppermute | solution.py:43
  212.5 41.8 %collective-permute-start.68 = (bf16[256,1024]{1,0:T(8,128)(2,1)S(1)}, bf16[256,1024]{1,0:T(8,128)(2,1)S(1)}, u32[]{:S(2)}, u32[]{:S(2)}) collective-permute-start(bf16[256,1024]{1,0:T(8,128)(2,1)S(1)} %copy-done.43), channel_id=1, source_target_pairs={{0,96},{4,100},{8,104},{12,108},{16,112},{20,116},{24,120},{28,124... | collective-permute-start | bytes 1572872 | tf_op jit(solution)/shard_map/ppermute | solution.py:43
  212.5 42.7 %collective-permute-start.67 = (bf16[256,1024]{1,0:T(8,128)(2,1)}, bf16[256,1024]{1,0:T(8,128)(2,1)S(1)}, u32[]{:S(2)}, u32[]{:S(2)}) collective-permute-start(bf16[256,1024]{1,0:T(8,128)(2,1)} %weight_grad.51), channel_id=1, source_target_pairs={{0,32},{4,36},{8,40},{12,44},{16,48},{20,52},{24,56},{28,60},{32,6... | collective-permute-start | bytes 1572872 | tf_op jit(solution)/shard_map/ppermute | solution.py:43
  224.1 51.7 %collective-permute-start.13 = (bf16[1024,512]{1,0:T(8,128)(2,1)}, bf16[1024,512]{1,0:T(8,128)(2,1)S(1)}, u32[]{:S(2)}, u32[]{:S(2)}) collective-permute-start(bf16[1024,512]{1,0:T(8,128)(2,1)} %get-tuple-element.33.kv), channel_id=1, source_target_pairs={{0,8},{4,12},{16,24},{20,28},{32,40},{36,44},{48,56},{52,60},{64,7... | collective-permute-start | bytes 3145736 | tf_op jit(solution)/shard_map/ppermute | solution.py:52
  230.9 25.1 %collective-permute-start.66 = (bf16[256,1024]{1,0:T(8,128)(2,1)}, bf16[256,1024]{1,0:T(8,128)(2,1)S(1)}, u32[]{:S(2)}, u32[]{:S(2)}) collective-permute-start(bf16[256,1024]{1,0:T(8,128)(2,1)} %weight_grad.49), channel_id=1, source_target_pairs={{0,64},{4,68},{8,72},{12,76},{16,80},{20,84},{24,88},{28,92},{32,9... | collective-permute-start | bytes 1572872 | tf_op jit(solution)/shard_map/ppermute | solution.py:43
  272.0 44.8 %collective-permute-start.76 = (bf16[512,1024]{1,0:T(8,128)(2,1)S(1)}, bf16[512,1024]{1,0:T(8,128)(2,1)S(1)}, u32[]{:S(2)}, u32[]{:S(2)}) collective-permute-start(bf16[512,1024]{1,0:T(8,128)(2,1)S(1)} %copy-done.32), channel_id=1, source_target_pairs={{0,24},{4,28},{8,16},{12,20},{16,0},{20,4},{24,8},{28,12},{32,56},... | collective-permute-start | bytes 3145736 | tf_op jit(solution)/shard_map/ppermute | solution.py:43
  273.4 46.8 %collective-permute-start.74 = (bf16[512,1024]{1,0:T(8,128)(2,1)}, bf16[512,1024]{1,0:T(8,128)(2,1)S(1)}, u32[]{:S(2)}, u32[]{:S(2)}) collective-permute-start(bf16[512,1024]{1,0:T(8,128)(2,1)} %weight_grad.55), channel_id=1, source_target_pairs={{0,16},{4,20},{8,24},{12,28},{16,8},{20,12},{24,0},{28,4},{32,48},... | collective-permute-start | bytes 3145736 | tf_op jit(solution)/shard_map/ppermute | solution.py:43
  274.0 63.6 %collective-permute-start.72 = (bf16[256,1024]{1,0:T(8,128)(2,1)S(1)}, bf16[256,1024]{1,0:T(8,128)(2,1)S(1)}, u32[]{:S(2)}, u32[]{:S(2)}) collective-permute-start(bf16[256,1024]{1,0:T(8,128)(2,1)S(1)} %add_convert_fusion.7), channel_id=1, source_target_pairs={{0,8},{4,12},{8,0},{12,4},{16,24},{20,28},{24,16},{28,20},{32,40},... | collective-permute-start | bytes 1572872 | tf_op jit(solution)/shard_map/ppermute | solution.py:43
  312.3 227.5 %collective-permute-start.28 = (bf16[512,2048]{1,0:T(8,128)(2,1)}, bf16[512,2048]{1,0:T(8,128)(2,1)S(1)}, u32[]{:S(2)}, u32[]{:S(2)}) collective-permute-start(bf16[512,2048]{1,0:T(8,128)(2,1)} %two_products.5), channel_id=1, source_target_pairs={{0,4},{4,0},{8,12},{12,8},{16,20},{20,16},{24,28},{28,24},{32,36},... | collective-permute-start | bytes 6291464 | tf_op jit(solution)/shard_map/ppermute | solution.py:43
  318.0 30.0 %collective-permute-start.78 = (bf16[256,1024]{1,0:T(8,128)(2,1)S(1)}, bf16[256,1024]{1,0:T(8,128)(2,1)S(1)}, u32[]{:S(2)}, u32[]{:S(2)}) collective-permute-start(bf16[256,1024]{1,0:T(8,128)(2,1)S(1)} %get-tuple-element.116), channel_id=1, source_target_pairs={{0,64},{4,68},{8,72},{12,76},{16,80},{20,84},{24,88},{28,92},{32,9... | collective-permute-start | bytes 1572872 | tf_op jit(solution)/shard_map/ppermute | solution.py:43
  318.4 31.0 %collective-permute-start.77 = (bf16[256,1024]{1,0:T(8,128)(2,1)}, bf16[256,1024]{1,0:T(8,128)(2,1)S(1)}, u32[]{:S(2)}, u32[]{:S(2)}) collective-permute-start(bf16[256,1024]{1,0:T(8,128)(2,1)} %get-tuple-element.115), channel_id=1, source_target_pairs={{0,96},{4,100},{8,104},{12,108},{16,112},{20,116},{24,120},{28,124... | collective-permute-start | bytes 1572872 | tf_op jit(solution)/shard_map/ppermute | solution.py:43
  320.4 29.0 %collective-permute-start.75 = (bf16[256,1024]{1,0:T(8,128)(2,1)S(1)}, bf16[256,1024]{1,0:T(8,128)(2,1)}, u32[]{:S(2)}, u32[]{:S(2)}) collective-permute-start(bf16[256,1024]{1,0:T(8,128)(2,1)S(1)} %add_convert_fusion.5), channel_id=1, source_target_pairs={{0,32},{4,36},{8,40},{12,44},{16,48},{20,52},{24,56},{28,60},{32,6... | collective-permute-start | bytes 1572872 | tf_op jit(solution)/shard_map/ppermute | solution.py:43
  337.9 37.3 %collective-permute-start.73 = (bf16[256,1024]{1,0:T(8,128)(2,1)S(1)}, bf16[256,1024]{1,0:T(8,128)(2,1)S(1)}, u32[]{:S(2)}, u32[]{:S(2)}) collective-permute-start(bf16[256,1024]{1,0:T(8,128)(2,1)S(1)} %add_convert_fusion.6), channel_id=1, source_target_pairs={{0,4},{4,0},{8,12},{12,8},{16,20},{20,16},{24,28},{28,24},{32,36},... | collective-permute-start | bytes 1572872 | tf_op jit(solution)/shard_map/ppermute | solution.py:43
  348.0 62.4 %collective-permute-start.35 = (bf16[1024,512]{1,0:T(8,128)(2,1)}, bf16[1024,512]{1,0:T(8,128)(2,1)S(1)}, u32[]{:S(2)}, u32[]{:S(2)}) collective-permute-start(bf16[1024,512]{1,0:T(8,128)(2,1)} %get-tuple-element.39), channel_id=1, source_target_pairs={{8,0},{12,4},{24,16},{28,20},{40,32},{44,36},{56,48},{60,52},{72,6... | collective-permute-start | bytes 3145736 | tf_op jit(solution)/shard_map/ppermute | solution.py:52
  350.9 57.5 %collective-permute-start.79 = (bf16[256,1024]{1,0:T(8,128)(2,1)S(1)}, bf16[256,1024]{1,0:T(8,128)(2,1)S(1)}, u32[]{:S(2)}, u32[]{:S(2)}) collective-permute-start(bf16[256,1024]{1,0:T(8,128)(2,1)S(1)} %add_convert_fusion.2), channel_id=1, source_target_pairs={{0,8},{4,12},{8,0},{12,4},{16,24},{20,28},{24,16},{28,20},{32,40},... | collective-permute-start | bytes 1572872 | tf_op jit(solution)/shard_map/ppermute | solution.py:43
  409.4 110.1 %collective-permute-start.80 = (bf16[256,1024]{1,0:T(8,128)(2,1)}, bf16[256,1024]{1,0:T(8,128)(2,1)}, u32[]{:S(2)}, u32[]{:S(2)}) collective-permute-start(bf16[256,1024]{1,0:T(8,128)(2,1)} %add_convert_fusion.1), channel_id=1, source_target_pairs={{0,4},{4,0},{8,12},{12,8},{16,20},{20,16},{24,28},{28,24},{32,36},... | collective-permute-start | bytes 1572872 | tf_op jit(solution)/shard_map/ppermute | solution.py:43
  441.9 28.2 %collective-permute-start.44 = (f32[2,2048]{1,0:T(2,128)S(1)}, f32[2,2048]{1,0:T(2,128)S(1)}, u32[]{:S(2)}, u32[]{:S(2)}) collective-permute-start(f32[2,2048]{1,0:T(2,128)S(1)} %pad_maximum_fusion.21), channel_id=1, source_target_pairs={{0,1},{1,2},{2,3},{3,0},{4,5},{5,6},{6,7},{7,4},{8,9},{9,10},{10,1... | collective-permute-start | bytes 49160 | tf_op jit(solution)/shard_map/ppermute | solution.py:56
  443.6 26.5 %collective-permute-start.45 = (f32[2,2048]{1,0:T(2,128)S(1)}, f32[2,2048]{1,0:T(2,128)S(1)}, u32[]{:S(2)}, u32[]{:S(2)}) collective-permute-start(f32[2,2048]{1,0:T(2,128)S(1)} %pad_maximum_fusion.21), channel_id=1, source_target_pairs={{0,3},{1,0},{2,1},{3,2},{4,7},{5,4},{6,5},{7,6},{8,11},{9,8},{10,9... | collective-permute-start | bytes 49160 | tf_op jit(solution)/shard_map/ppermute | solution.py:56
  445.9 24.2 %collective-permute-start.43 = (f32[2,2048]{1,0:T(2,128)S(1)}, f32[2,2048]{1,0:T(2,128)S(1)}, u32[]{:S(2)}, u32[]{:S(2)}) collective-permute-start(f32[2,2048]{1,0:T(2,128)S(1)} %pad_maximum_fusion.21), channel_id=1, source_target_pairs={{0,2},{1,3},{2,0},{3,1},{4,6},{5,7},{6,4},{7,5},{8,10},{9,11},{10,... | collective-permute-start | bytes 49160 | tf_op jit(solution)/shard_map/ppermute | solution.py:56
  487.2 26.7 %collective-permute-start.57 = (bf16[256,1024]{1,0:T(8,128)(2,1)}, bf16[256,1024]{1,0:T(8,128)(2,1)S(1)}, u32[]{:S(2)}, u32[]{:S(2)}) collective-permute-start(bf16[256,1024]{1,0:T(8,128)(2,1)} %pad_maximum_fusion.8), channel_id=1, source_target_pairs={{0,96},{4,100},{8,104},{12,108},{16,112},{20,116},{24,120},{28,124... | collective-permute-start | bytes 1572872 | tf_op jit(solution)/shard_map/ppermute | solution.py:43
  492.5 25.3 %collective-permute-start.56 = (bf16[256,1024]{1,0:T(8,128)(2,1)}, bf16[256,1024]{1,0:T(8,128)(2,1)}, u32[]{:S(2)}, u32[]{:S(2)}) collective-permute-start(bf16[256,1024]{1,0:T(8,128)(2,1)} %pad_maximum_fusion.7), channel_id=1, source_target_pairs={{0,32},{4,36},{8,40},{12,44},{16,48},{20,52},{24,56},{28,60},{32,6... | collective-permute-start | bytes 1572872 | tf_op jit(solution)/shard_map/ppermute | solution.py:43
  500.5 22.6 %collective-permute-start.55 = (bf16[256,1024]{1,0:T(8,128)(2,1)}, bf16[256,1024]{1,0:T(8,128)(2,1)}, u32[]{:S(2)}, u32[]{:S(2)}) collective-permute-start(bf16[256,1024]{1,0:T(8,128)(2,1)} %pad_maximum_fusion.6), channel_id=1, source_target_pairs={{0,64},{4,68},{8,72},{12,76},{16,80},{20,84},{24,88},{28,92},{32,9... | collective-permute-start | bytes 1572872 | tf_op jit(solution)/shard_map/ppermute | solution.py:43
  533.9 55.2 %collective-permute-start.36 = (bf16[512,2048]{1,0:T(8,128)(2,1)}, bf16[512,2048]{1,0:T(8,128)(2,1)}, u32[]{:S(2)}, u32[]{:S(2)}) collective-permute-start(bf16[512,2048]{1,0:T(8,128)(2,1)} %two_products.7.a), channel_id=1, source_target_pairs={{0,4},{4,0},{8,12},{12,8},{16,20},{20,16},{24,28},{28,24},{32,36},... | collective-permute-start | bytes 6291464 | tf_op jit(solution)/shard_map/ppermute | solution.py:43
  542.4 23.2 %collective-permute-start.30 = (bf16[128,2048]{1,0:T(8,128)(2,1)}, bf16[128,2048]{1,0:T(8,128)(2,1)}, u32[]{:S(2)}, u32[]{:S(2)}) collective-permute-start(bf16[128,2048]{1,0:T(8,128)(2,1)} %get-tuple-element.106), channel_id=1, source_target_pairs={{0,2},{1,3},{2,0},{3,1},{4,6},{5,7},{6,4},{7,5},{8,10},{9,11},{10,... | collective-permute-start | bytes 1572872 | tf_op jit(solution)/shard_map/ppermute | solution.py:56
  543.2 24.6 %collective-permute-start.31 = (bf16[128,2048]{1,0:T(8,128)(2,1)}, bf16[128,2048]{1,0:T(8,128)(2,1)}, u32[]{:S(2)}, u32[]{:S(2)}) collective-permute-start(bf16[128,2048]{1,0:T(8,128)(2,1)} %get-tuple-element.105), channel_id=1, source_target_pairs={{0,3},{1,0},{2,1},{3,2},{4,7},{5,4},{6,5},{7,6},{8,11},{9,8},{10,9... | collective-permute-start | bytes 1572872 | tf_op jit(solution)/shard_map/ppermute | solution.py:56
  552.6 24.6 %collective-permute-start.62 = (bf16[1,256,1024]{2,1,0:T(8,128)(2,1)S(1)}, bf16[1,256,1024]{2,1,0:T(8,128)(2,1)}, u32[]{:S(2)}, u32[]{:S(2)}) collective-permute-start(bf16[1,256,1024]{2,1,0:T(8,128)(2,1)S(1)} %fusion.4), channel_id=1, source_target_pairs={{0,4},{4,0},{8,12},{12,8},{16,20},{20,16},{24,28},{28,24},{32,36},... | collective-permute-start | bytes 1572872 | tf_op jit(solution)/shard_map/ppermute | solution.py:43
  571.8 36.9 %collective-permute-start.32 = (bf16[128,2048]{1,0:T(8,128)(2,1)}, bf16[128,2048]{1,0:T(8,128)(2,1)}, u32[]{:S(2)}, u32[]{:S(2)}) collective-permute-start(bf16[128,2048]{1,0:T(8,128)(2,1)} %forward_rows.1), channel_id=1, source_target_pairs={{0,3},{1,0},{2,1},{3,2},{4,7},{5,4},{6,5},{7,6},{8,11},{9,8},{10,9... | collective-permute-start | bytes 1572872 | tf_op jit(solution)/shard_map/ppermute | solution.py:56
  575.3 38.1 %collective-permute-start.33 = (bf16[128,2048]{1,0:T(8,128)(2,1)}, bf16[128,2048]{1,0:T(8,128)(2,1)}, u32[]{:S(2)}, u32[]{:S(2)}) collective-permute-start(bf16[128,2048]{1,0:T(8,128)(2,1)} %forward_rows.1), channel_id=1, source_target_pairs={{0,2},{1,3},{2,0},{3,1},{4,6},{5,7},{6,4},{7,5},{8,10},{9,11},{10,... | collective-permute-start | bytes 1572872 | tf_op jit(solution)/shard_map/ppermute | solution.py:56
  575.6 55.3 %collective-permute-start.34 = (bf16[128,2048]{1,0:T(8,128)(2,1)}, bf16[128,2048]{1,0:T(8,128)(2,1)}, u32[]{:S(2)}, u32[]{:S(2)}) collective-permute-start(bf16[128,2048]{1,0:T(8,128)(2,1)} %forward_rows.1), channel_id=1, source_target_pairs={{0,1},{1,2},{2,3},{3,0},{4,5},{5,6},{6,7},{7,4},{8,9},{9,10},{10,1... | collective-permute-start | bytes 1572872 | tf_op jit(solution)/shard_map/ppermute | solution.py:56
  592.4 22.1 %collective-permute-start.37 = (bf16[128,2048]{1,0:T(8,128)(2,1)S(1)}, bf16[128,2048]{1,0:T(8,128)(2,1)S(1)}, u32[]{:S(2)}, u32[]{:S(2)}) collective-permute-start(bf16[128,2048]{1,0:T(8,128)(2,1)S(1)} %get-tuple-element.103), channel_id=1, source_target_pairs={{0,1},{1,2},{2,3},{3,0},{4,5},{5,6},{6,7},{7,4},{8,9},{9,10},{10,1... | collective-permute-start | bytes 1572872 | tf_op jit(solution)/shard_map/ppermute | solution.py:56
  594.5 28.9 %collective-permute-start.38 = (bf16[128,2048]{1,0:T(8,128)(2,1)S(1)}, bf16[128,2048]{1,0:T(8,128)(2,1)S(1)}, u32[]{:S(2)}, u32[]{:S(2)}) collective-permute-start(bf16[128,2048]{1,0:T(8,128)(2,1)S(1)} %get-tuple-element.102), channel_id=1, source_target_pairs={{0,2},{1,3},{2,0},{3,1},{4,6},{5,7},{6,4},{7,5},{8,10},{9,11},{10,... | collective-permute-start | bytes 1572872 | tf_op jit(solution)/shard_map/ppermute | solution.py:56
  632.1 26.4 %collective-permute-start.42 = (bf16[128,2048]{1,0:T(8,128)(2,1)}, bf16[128,2048]{1,0:T(8,128)(2,1)S(1)}, u32[]{:S(2)}, u32[]{:S(2)}) collective-permute-start(bf16[128,2048]{1,0:T(8,128)(2,1)} %backward_rows.1), channel_id=1, source_target_pairs={{0,1},{1,2},{2,3},{3,0},{4,5},{5,6},{6,7},{7,4},{8,9},{9,10},{10,1... | collective-permute-start | bytes 1572872 | tf_op jit(solution)/shard_map/ppermute | solution.py:56
  (87 other events, 1102.4 us)

commit v2 on v1

--- a/solution.py
+++ b/solution.py
@@ -56,13 +56,6 @@
     return lax.ppermute(arr, "tp", [(i, (i + dz) % 4) for i in range(4)])
 
 
-def gather_weight(shard):
-    r3, r1, r2 = plane(shard, dy=1), plane(shard, dy=-1), plane(shard, dy=2)
-    s0 = plane(shard, dx=1)
-    s1, s2, s3 = plane(r1, dx=1), plane(r2, dx=-1), plane(r3, dx=-1)
-    return jnp.concatenate([shard, r1, r2, r3, s0, s1, s2, s3], axis=0)
-
-
 def add_low(*parts):
     total = parts[0].astype(F32)
     for part in parts[1:]:
@@ -99,97 +92,11 @@
     return lax.rem(y + dy, 4) * 2 + lax.rem(x_lo + dx, 2)
 
 
-def prep_kernel(place, tok, grad, gain, shift, normed, normed_t, unit, grad_rel, grad_t, bias_grad, full, full_u):
-    y, x_lo = place[0], place[1]
-    rows = tok[...].astype(F32)
-    mean = jnp.mean(rows, axis=-1, keepdims=True)
-    centered = rows - mean
-    inv = lax.rsqrt(jnp.mean(centered * centered, axis=-1, keepdims=True) + EPSILON)
-    unit_rows = centered * inv
-    full_u[...] = unit_rows
-    full[...] = unit_rows * gain[...] + shift[...]
-
-    @pl.when(pl.program_id(0) == 0)
-    def _():
-        bias_grad[...] = jnp.zeros_like(bias_grad)
-
-    for j in range(8):
-        src = pl.ds(pl.multiple_of(block_order(y, x_lo, j) * BLK, BLK), BLK)
-        dst = pl.ds(j * BLK, BLK)
-        part = full[:, src]
-        normed[:, dst] = part.astype(BF16)
-        normed_t[dst, :] = part.T.astype(BF16)
-        unit[:, dst] = full_u[:, src].astype(BF16)
-        g = grad[:, src]
-        g32 = g.astype(F32)
-        grad_rel[:, dst] = g
-        grad_t[dst, :] = g32.T.astype(BF16)
-        bias_grad[:, dst] += jnp.sum(g32, axis=0, keepdims=True)
-
-
-def prep(place, tok, grad, gain, shift):
-    tile = 256
-    rows = pl.BlockSpec((tile, D), lambda i, p: (i, 0))
-    cols = pl.BlockSpec((D, tile), lambda i, p: (0, i))
-    vec = pl.BlockSpec((1, D), lambda i, p: (0, 0))
-    return pl.pallas_call(
-        prep_kernel,
-        grid_spec=pltpu.PrefetchScalarGridSpec(
-            num_scalar_prefetch=1,
-            grid=(ROWS // tile,),
-            in_specs=[rows, rows, vec, vec],
-            out_specs=[rows, cols, rows, rows, cols, vec],
-            scratch_shapes=[pltpu.VMEM((tile, D), F32), pltpu.VMEM((tile, D), F32)],
-        ),
-        out_shape=[
-            jax.ShapeDtypeStruct((ROWS, D), BF16),
-            jax.ShapeDtypeStruct((D, ROWS), BF16),
-            jax.ShapeDtypeStruct((ROWS, D), BF16),
-            jax.ShapeDtypeStruct((ROWS, D), BF16),
-            jax.ShapeDtypeStruct((D, ROWS), BF16),
-            jax.ShapeDtypeStruct((1, D), F32),
-        ],
-        compiler_params=params(),
-        cost_estimate=cost(40 * ROWS * D, 14 * ROWS * D),
-        name="prep",
-    )(place, tok, grad, gain, shift)
-
-
 def partner(v):
     lane = lax.broadcasted_iota(jnp.int32, v.shape, 1)
     up = pltpu.roll(v, v.shape[1] - ROT // 2, 1)
     down = pltpu.roll(v, ROT // 2, 1)
     return jnp.where(lane % HD < ROT // 2, up, down)
-
-
-def qkv_kernel(normed, grad, w, bias, cos, sin, q, kv, do):
-    raw = jnp.dot(normed[...], w[:, : 3 * BLK], preferred_element_type=F32) + bias[...]
-    c, s = cos[...], sin[...]
-    qr, kr = raw[:, :BLK], raw[:, BLK : 2 * BLK]
-    q[...] = ((qr * c + partner(qr) * s).astype(BF16).astype(F32) * (HD**-0.5)).astype(BF16)
-    kv[:, :BLK] = (kr * c + partner(kr) * s).astype(BF16)
-    kv[:, BLK:] = raw[:, 2 * BLK :].astype(BF16)
-    do[...] = jnp.dot(grad[...], w[:, 3 * BLK :], preferred_element_type=F32).astype(BF16)
-
-
-def qkv_call(normed, grad, w, bias, cos, sin):
-    tile = 256
-    rows = lambda n: pl.BlockSpec((tile, n), lambda i: (i, 0))
-    fixed = lambda a, b: pl.BlockSpec((a, b), lambda i: (0, 0))
-    return pl.pallas_call(
-        qkv_kernel,
-        grid=(ROWS // tile,),
-        in_specs=[rows(D), rows(D), fixed(D, 4 * BLK), fixed(1, 3 * BLK), rows(BLK), rows(BLK)],
-        out_specs=[rows(BLK), rows(2 * BLK), rows(BLK)],
-        out_shape=[
-            jax.ShapeDtypeStruct((ROWS, BLK), BF16),
-            jax.ShapeDtypeStruct((ROWS, 2 * BLK), BF16),
-            jax.ShapeDtypeStruct((ROWS, BLK), BF16),
-        ],
-        compiler_params=params(),
-        cost_estimate=cost(2 * ROWS * D * 4 * BLK, 16 * ROWS * D),
-        name="qkv",
-    )(normed, grad, w, bias, cos, sin)
 
 
 QT = 512
@@ -344,61 +251,6 @@
 GELU_C = math.sqrt(2.0 / math.pi)
 
 
-def fc1_kernel(normed, w, bias, active, slope):
-    v = jnp.dot(normed[...], w[...], preferred_element_type=F32) + bias[...]
-    sq = v * v
-    t = jnp.tanh(GELU_C * v * (1.0 + 0.044715 * sq))
-    half = 0.5 * (1.0 + t)
-    active[...] = (v * half).astype(BF16)
-    slope[...] = (half + 0.5 * v * (1.0 - t * t) * (GELU_C * (1.0 + 3 * 0.044715 * sq))).astype(BF16)
-
-
-def fc1_call(normed, w, bias):
-    tile = 256
-    n = w.shape[1]
-    rows = lambda m: pl.BlockSpec((tile, m), lambda i: (i, 0))
-    fixed = lambda a, b: pl.BlockSpec((a, b), lambda i: (0, 0))
-    return pl.pallas_call(
-        fc1_kernel,
-        grid=(ROWS // tile,),
-        in_specs=[rows(D), fixed(D, n), fixed(1, n)],
-        out_specs=[rows(n), rows(n)],
-        out_shape=[jax.ShapeDtypeStruct((ROWS, n), BF16)] * 2,
-        compiler_params=params(),
-        cost_estimate=cost(2 * ROWS * D * n, 2 * (ROWS * D + D * n + 2 * ROWS * n), ROWS * n),
-        name="fc1",
-    )(normed, w, bias)
-
-
-def hidden_grad_kernel(grad, w, slope, out, bias_grad):
-    v = jnp.dot(grad[...], w[...], preferred_element_type=F32) * slope[...].astype(F32)
-    low = v.astype(BF16)
-    out[...] = low
-
-    @pl.when(pl.program_id(0) == 0)
-    def _():
-        bias_grad[...] = jnp.zeros_like(bias_grad)
-
-    bias_grad[...] += jnp.sum(low.astype(F32), axis=0, keepdims=True)
-
-
-def hidden_grad_call(grad, w, slope):
-    tile = 256
-    n = w.shape[1]
-    rows = lambda m: pl.BlockSpec((tile, m), lambda i: (i, 0))
-    fixed = lambda a, b: pl.BlockSpec((a, b), lambda i: (0, 0))
-    return pl.pallas_call(
-        hidden_grad_kernel,
-        grid=(ROWS // tile,),
-        in_specs=[rows(D), fixed(D, n), rows(n)],
-        out_specs=[rows(n), fixed(1, n)],
-        out_shape=[jax.ShapeDtypeStruct((ROWS, n), BF16), jax.ShapeDtypeStruct((1, n), F32)],
-        compiler_params=params(),
-        cost_estimate=cost(2 * ROWS * D * n, 2 * (ROWS * D + D * n + 2 * ROWS * n)),
-        name="hidden_grad",
-    )(grad, w, slope)
-
-
 def weight_grad_kernel(left, *refs):
     out = refs[-1]
     at = 0
@@ -558,63 +410,290 @@
     return out
 
 
+MESH = pl.DeviceIdType.MESH
+PACK = 24
+
+
+def coords():
+    f, c, z = lax.axis_index("fsdp"), lax.axis_index("ctx"), lax.axis_index("tp")
+    return (c // 2) * 2 + f % 2, f // 2, z, c % 2
+
+
+def device(x, y, z, core):
+    return (y * 2 + lax.rem(x, 2), (x // 2) * 2 + core, z)
+
+
+def beside(dx=0, dy=0, flip=0, dz=0):
+    x, y, z, core = coords()
+    return device(
+        lax.rem(x + dx + 4, 4), lax.rem(y + dy + 4, 4), lax.rem(z + dz + 4, 4), (1 - core) if flip else core
+    )
+
+
+def greet(targets):
+    barrier = pltpu.get_barrier_semaphore()
+    for target in targets:
+        pl.semaphore_signal(barrier, inc=1, device_id=target, device_id_type=MESH)
+    pl.semaphore_wait(barrier, len(targets))
+
+
+def gather_kernel(s1, s2, s3, tok_in, grad_in, pack, cos_in, sin_in,
+                  w1_out, w2_out, w3_out, normed_t_out, grad_t_out, unit_out, q_out, kv_out, kvr_out, do_out,
+                  active_out, hidden_out, small_out, bias_out, up_bias_out,
+                  w1, w2, w3, tok, grad, normed, grad_rel, normed_t, grad_t, unit, small, q, kv, do, active, slope,
+                  hidden, cos, sin, bias_sum, up_bias_sum, send, recv, local):
+    x, y, z, core = coords()
+    x_lo, x_hi = lax.rem(x, 2), x // 2
+    greet([beside(dy=1), beside(dy=3), beside(dy=2), beside(dx=1), beside(dx=3), beside(dx=2), beside(flip=1)])
+
+    def remote(i, src, dst, target):
+        copy = pltpu.make_async_remote_copy(src, dst, send.at[i], recv.at[i], device_id=target, device_id_type=MESH)
+        copy.start()
+        return copy
+
+    def here(i, src, dst):
+        copy = pltpu.make_async_copy(src, dst, local.at[i])
+        copy.start()
+        return copy
+
+    shards, gathered = (s1, s2, s3), (w1, w2, w3)
+    block = lambda w, j: w.at[pl.ds(j * BLK, BLK)]
+    top = lambda w, j: w.at[pl.ds(j * BLK, BLK // 2)]
+    bottom = lambda w, j: w.at[pl.ds(j * BLK + BLK // 2, BLK // 2)]
+
+    def first_stage(g):
+        s, w, at = shards[g], gathered[g], 8 + 9 * g
+        own = here(g, s, block(w, 0))
+        along_y = [
+            remote(at, s, block(w, 3), beside(dy=1)),
+            remote(at + 1, s, block(w, 1), beside(dy=3)),
+            remote(at + 2, s, block(w, 2), beside(dy=2)),
+        ]
+        along_x = [
+            remote(at + 3, s.at[pl.ds(0, BLK // 2)], top(w, 4), beside(dx=1)),
+            remote(at + 4, s.at[pl.ds(BLK // 2, BLK // 2)], bottom(w, 4), beside(dx=3)),
+        ]
+        return own, along_y, along_x
+
+    def second_stage(g, along_y):
+        w, at = gathered[g], 8 + 9 * g + 5
+        for copy in along_y:
+            copy.wait_recv()
+        return [
+            remote(at, block(w, 1), block(w, 5), beside(dx=1)),
+            remote(at + 1, block(w, 3), block(w, 7), beside(dx=3)),
+            remote(at + 2, top(w, 2), top(w, 6), beside(dx=1)),
+            remote(at + 3, bottom(w, 2), bottom(w, 6), beside(dx=3)),
+        ]
+
+    def arrived(own, along_x, second):
+        own.wait()
+        for copy in along_x + second:
+            copy.wait_recv()
+
+    my_rows = pl.ds(pl.multiple_of(core * HALF, HALF), HALF)
+    pack_y = [
+        remote(0, pack, small.at[3], beside(dy=1)),
+        remote(1, pack, small.at[1], beside(dy=3)),
+        remote(2, pack, small.at[2], beside(dy=2)),
+    ]
+    pack_own = here(3, pack, small.at[0])
+    tok_copy = remote(4, tok_in, tok.at[my_rows], beside(flip=1))
+    grad_copy = remote(5, grad_in, grad.at[my_rows], beside(flip=1))
+    mine = [here(4, tok_in, tok.at[my_rows]), here(5, grad_in, grad.at[my_rows]), here(6, cos_in, cos), here(7, sin_in, sin)]
+    own1, y1, x1 = first_stage(0)
+    for copy in pack_y:
+        copy.wait_recv()
+    pack_own.wait()
+    pack_x = remote(3, small.at[pl.ds(0, 4)], small.at[pl.ds(4, 4)], beside(dx=1))
+    for copy in mine:
+        copy.wait()
+    tok_copy.wait_recv()
+    grad_copy.wait_recv()
+    pack_x.wait_recv()
+
+    bias_sum[...] = jnp.zeros_like(bias_sum)
+    up_bias_sum[...] = jnp.zeros_like(up_bias_sum)
+    tile = 128
+
+    @pl.loop(0, ROWS // tile)
+    def _(i):
+        at = pl.ds(pl.multiple_of(i * tile, tile), tile)
+        rows = tok[at, :].astype(F32)
+        mean = jnp.mean(rows, axis=-1, keepdims=True)
+        centered = rows - mean
+        inv = lax.rsqrt(jnp.mean(centered * centered, axis=-1, keepdims=True) + EPSILON)
+        for j in range(8):
+            src = pl.ds(pl.multiple_of(block_order(y, x_lo, j) * BLK, BLK), BLK)
+            dst = pl.ds(j * BLK, BLK)
+            gain = jnp.concatenate([small[j, 0:1, :], small[j, 1:2, :]], axis=1)
+            shift = jnp.concatenate([small[j, 2:3, :], small[j, 3:4, :]], axis=1)
+            u = (tok[at, src].astype(F32) - mean) * inv
+            n = u * gain + shift
+            normed[at, dst] = n.astype(BF16)
+            normed_t[dst, at] = n.T.astype(BF16)
+            unit[at, dst] = u.astype(BF16)
+            g = grad[at, src]
+            g32 = g.astype(F32)
+            grad_rel[at, dst] = g
+            grad_t[dst, at] = g32.T.astype(BF16)
+            bias_sum[:, dst] += jnp.sum(g32, axis=0, keepdims=True)
+
+    saved = [here(8, normed_t, normed_t_out), here(9, grad_t, grad_t_out), here(10, unit, unit_out), here(11, small, small_out),
+             here(12, bias_sum, bias_out)]
+    second1 = second_stage(0, y1)
+    own2, y2, x2 = first_stage(1)
+    arrived(own1, x1, second1)
+    second2 = second_stage(1, y2)
+    own3, y3, x3 = first_stage(2)
+    saved.append(here(13, w1, w1_out))
+
+    biases = small[0, 6:20, :]
+    for j in range(1, 8):
+        biases = biases + small[j, 6:20, :]
+    qkv_bias = jnp.concatenate([biases[j : j + 1] for j in range(6)], axis=1)
+    up_bias = jnp.concatenate([biases[j : j + 1] for j in range(6, 14)], axis=1)
+    big = 256
+
+    @pl.loop(0, ROWS // big)
+    def _(i):
+        at = pl.ds(pl.multiple_of(i * big, big), big)
+        raw = jnp.dot(normed[at, :], w1[:, : 3 * BLK], preferred_element_type=F32) + qkv_bias
+        c, s = cos[at, :], sin[at, :]
+        qr, kr = raw[:, :BLK], raw[:, BLK : 2 * BLK]
+        q[at, :] = ((qr * c + partner(qr) * s).astype(BF16).astype(F32) * (HD**-0.5)).astype(BF16)
+        kv[at, :BLK] = (kr * c + partner(kr) * s).astype(BF16)
+        kv[at, BLK:] = raw[:, 2 * BLK :].astype(BF16)
+        do[at, :] = jnp.dot(grad_rel[at, :], w1[:, 3 * BLK :], preferred_element_type=F32).astype(BF16)
+
+    kv_copy = pltpu.make_async_remote_copy(
+        kv, kvr_out, send.at[6], recv.at[6], device_id=beside(dx=2), device_id_type=MESH
+    )
+
+    @pl.when(x_hi == 0)
+    def _():
+        kv_copy.start()
+
+    saved += [here(14, q, q_out), here(15, kv, kv_out), here(16, do, do_out)]
+    arrived(own2, x2, second2)
+    second3 = second_stage(2, y3)
+    saved.append(here(17, w2, w2_out))
+
+    @pl.loop(0, ROWS // big)
+    def _(i):
+        at = pl.ds(pl.multiple_of(i * big, big), big)
+        v = jnp.dot(normed[at, :], w2[...], preferred_element_type=F32) + up_bias
+        sq = v * v
+        t = jnp.tanh(GELU_C * v * (1.0 + 0.044715 * sq))
+        half = 0.5 * (1.0 + t)
+        active[at, :] = (v * half).astype(BF16)
+        slope[at, :] = (half + 0.5 * v * (1.0 - t * t) * (GELU_C * (1.0 + 3 * 0.044715 * sq))).astype(BF16)
+
+    saved.append(here(18, active, active_out))
+    arrived(own3, x3, second3)
+    saved.append(here(19, w3, w3_out))
+
+    @pl.loop(0, ROWS // big)
+    def _(i):
+        at = pl.ds(pl.multiple_of(i * big, big), big)
+        v = jnp.dot(grad_rel[at, :], w3[...], preferred_element_type=F32) * slope[at, :].astype(F32)
+        low = v.astype(BF16)
+        hidden[at, :] = low
+        up_bias_sum[...] += jnp.sum(low.astype(F32), axis=0, keepdims=True)
+
+    saved += [here(20, hidden, hidden_out), here(21, up_bias_sum, up_bias_out)]
+    for copy in pack_y + [pack_x, tok_copy, grad_copy] + y1 + x1 + second1 + y2 + x2 + second2 + y3 + x3 + second3:
+        copy.wait_send()
+
+    @pl.when(x_hi == 0)
+    def _():
+        kv_copy.wait_send()
+
+    @pl.when(x_hi == 1)
+    def _():
+        kv_copy.wait_recv()
+
+    for copy in saved:
+        copy.wait()
+
+
+def gather_call(s1, s2, s3, tok, grad, pack, cos, sin):
+    n = 1024
+    low = lambda *shape: jax.ShapeDtypeStruct(shape, BF16)
+    wide = lambda *shape: jax.ShapeDtypeStruct(shape, F32)
+    vlow = lambda *shape: pltpu.VMEM(shape, BF16)
+    vwide = lambda *shape: pltpu.VMEM(shape, F32)
+    anywhere = pl.BlockSpec(memory_space=pl.ANY)
+    return pl.pallas_call(
+        gather_kernel,
+        in_specs=[anywhere] * 8,
+        out_specs=[anywhere] * 15,
+        out_shape=[
+            low(D, n), low(D, n), low(D, n), low(D, ROWS), low(D, ROWS), low(ROWS, D), low(ROWS, BLK), low(ROWS, 2 * BLK),
+            low(ROWS, 2 * BLK), low(ROWS, BLK), low(ROWS, n), low(ROWS, n), wide(8, PACK, 128), wide(1, D), wide(1, n),
+        ],
+        scratch_shapes=[
+            vlow(D, n), vlow(D, n), vlow(D, n), vlow(ROWS, D), vlow(ROWS, D), vlow(ROWS, D), vlow(ROWS, D), vlow(D, ROWS),
+            vlow(D, ROWS), vlow(ROWS, D), vwide(8, PACK, 128), vlow(ROWS, BLK), vlow(ROWS, 2 * BLK), vlow(ROWS, BLK),
+            vlow(ROWS, n), vlow(ROWS, n), vlow(ROWS, n), vwide(ROWS, BLK), vwide(ROWS, BLK), vwide(1, D), vwide(1, n),
+            pltpu.SemaphoreType.DMA((35,)),
+            pltpu.SemaphoreType.DMA((35,)),
+            pltpu.SemaphoreType.DMA((22,)),
+        ],
+        compiler_params=params(collective_id=0, has_side_effects=True),
+        cost_estimate=cost(2 * ROWS * D * 3 * n, 64 * 1024 * 1024),
+        name="gather_phase",
+    )(s1, s2, s3, tok, grad, pack, cos, sin)
+
+
 def body(tokens, ln_gain, ln_shift, out_bias, w_qkv, b_qkv, w_out, w_fc1, b_fc1, w_fc2, out_grad):
     f, c, z = lax.axis_index("fsdp"), lax.axis_index("ctx"), lax.axis_index("tp")
     y, x_lo, x_hi, core = f // 2, f % 2, c // 2, c % 2
     place = jnp.stack([y, x_lo, x_hi, core, z]).astype(jnp.int32)
     tokens, out_grad = tokens[0], out_grad[0]
 
-    def pair(mine):
-        other = plane(mine, flip=1)
-        first = core == 0
-        return jnp.concatenate([jnp.where(first, mine, other), jnp.where(first, other, mine)], axis=0)
-
+    qkv_shard = lax.dynamic_slice_in_dim(w_qkv, core * BLK, BLK, axis=2).reshape(BLK, 3 * BLK)
+    proj_shard = lax.dynamic_slice_in_dim(w_out, core * BLK, BLK, axis=0).T
+    attn_shard = jnp.concatenate([qkv_shard, proj_shard], axis=1)
+    up_shard = lax.dynamic_slice_in_dim(w_fc1, core * 1024, 1024, axis=1)
+    down_shard = lax.dynamic_slice_in_dim(w_fc2, core * 1024, 1024, axis=0).T
+
+    own = (jnp.arange(HD) // 8 == f)[None, None, :]
+    spread = lambda v: jnp.where(own, jnp.tile(v, (1, 1, 8)), jnp.zeros((), BF16)).reshape(-1)
     pack = jnp.concatenate(
-        [ln_gain, ln_shift, out_bias, b_qkv.reshape(-1), b_fc1.reshape(-1), jnp.zeros((64,), BF16)]
-    ).reshape(10, 128)
-    small = jnp.stack([pack, plane(pack, dy=-1), plane(pack, dy=2), plane(pack, dy=1)])
-    small = jnp.concatenate([small, plane(small, dx=1)]).reshape(8, 1280)
+        [
+            ln_gain,
+            ln_shift,
+            out_bias,
+            spread(lax.dynamic_slice_in_dim(b_qkv, core * 4, 4, axis=1)),
+            spread(lax.dynamic_slice_in_dim(b_fc1, core * 16, 16, axis=0)[None]),
+            jnp.zeros((512,), BF16),
+        ]
+    )
+    pack = pack.astype(F32).reshape(PACK, 128)
+
+    lane = jnp.arange(BLK, dtype=jnp.int32) % HD
+    freq = jnp.where(lane < ROT, 10000.0 ** (-2.0 * (lane % (ROT // 2)).astype(F32) / ROT), 0.0)
+    sign = jnp.where(lane < ROT // 2, -1.0, 1.0)
+
+    def tables(first):
+        angle = (first + jnp.arange(ROWS, dtype=jnp.int32)).astype(F32)[:, None] * freq[None, :]
+        return jnp.cos(angle), jnp.sin(angle) * sign[None, :]
+
+    cos_r, sin_r = tables(0)
+    cos, sin = tables(x_hi * ROWS)
+
+    (w_attn, w_up, w_down, normed_t, grad_t, unit, q, kv, kvr, do, active, hidden_grad, small, bias_grad, up_bias_grad) = (
+        gather_call(attn_shard, up_shard, down_shard, tokens, out_grad, pack, cos, sin)
+    )
     order = jnp.stack([block_order(y, x_lo, j) for j in range(8)])
     where_is = jnp.sum(
         jnp.where(order[None, :] == jnp.arange(8)[:, None], jnp.arange(8)[None, :], 0), axis=1
     )
-    small = jnp.take(small, where_is, axis=0)
-    gain = small[:, :256].reshape(1, D).astype(F32)
-    shift = small[:, 256:512].reshape(1, D).astype(F32)
-    bias = small[:, 512:768].reshape(1, D).astype(F32)
-    qkv_bias = small[:, 768:960].reshape(8, 3, 8, 8).transpose(1, 2, 0, 3).astype(F32)
-    qkv_bias = lax.dynamic_slice_in_dim(qkv_bias, core * 4, 4, axis=1).reshape(1, 3 * BLK)
-    up_bias = small[:, 960:1216].reshape(8, 32, 8).transpose(1, 0, 2).astype(F32)
-    up_bias = lax.dynamic_slice_in_dim(up_bias, core * 16, 16, axis=0).reshape(1, 1024)
-
-    tok = pair(tokens)
-    grad = pair(out_grad)
-    qkv_shard = lax.dynamic_slice_in_dim(w_qkv, core * BLK, BLK, axis=2).reshape(BLK, 3 * BLK)
-    proj_shard = lax.dynamic_slice_in_dim(w_out, core * BLK, BLK, axis=0).T
-    up_shard = lax.dynamic_slice_in_dim(w_fc1, core * 1024, 1024, axis=1)
-    down_shard = lax.dynamic_slice_in_dim(w_fc2, core * 1024, 1024, axis=0).T
-    w_attn = gather_weight(jnp.concatenate([qkv_shard, proj_shard], axis=1))
-    w_up = gather_weight(up_shard)
-    w_down = gather_weight(down_shard)
-
-    lane = jnp.arange(BLK, dtype=jnp.int32) % HD
-    freq = jnp.where(lane < ROT, 10000.0 ** (-2.0 * (lane % (ROT // 2)).astype(F32) / ROT), 0.0)
-    sign = jnp.where(lane < ROT // 2, -1.0, 1.0)
-
-    def tables(first):
-        angle = (first + jnp.arange(ROWS, dtype=jnp.int32)).astype(F32)[:, None] * freq[None, :]
-        return jnp.cos(angle), jnp.sin(angle) * sign[None, :]
-
-    cos_r, sin_r = tables(0)
-    cos, sin = tables(x_hi * ROWS)
-
-    normed, normed_t, unit, grad_rel, grad_t, bias_grad = prep(place, tok, grad, gain, shift)
-    q, kv, do = qkv_call(normed, grad_rel, w_attn, qkv_bias, cos, sin)
-    kvr = across(kv, True)
-
-    active, slope = fc1_call(normed, w_up, up_bias)
+    small = jnp.take(small.reshape(8, PACK * 128)[:, : 3 * BLK], where_is, axis=0)
+    gain = small[:, :BLK].reshape(1, D)
+    bias = small[:, 2 * BLK :].reshape(1, D)
     down_piece = reduce_x_first(weight_grad(grad_t, active))
-    hidden_grad, up_bias_grad = hidden_grad_call(grad_rel, w_down, slope)
     up_piece = reduce_y_first(weight_grad(normed_t, hidden_grad))
 
     att, dq, dkv, dkvr = attention(place, q, kv, kvr, do, cos, sin, cos_r, sin_r)

time: 672 us -> 608 us (0.905)
  waiting for transfers between devices: 197 us -> 112 us
  Pallas kernels: 214 us -> 292 us
  local copies, waits for them, and re-layouts: 58.1 us -> 27.8 us
  starting transfers between devices: 144 us -> 122 us
    ppermute x64 -> x37, waiting for transfers between devices: 138 us -> 44.1 us  [plane(): return lax.ppermute(arr, ('fsdp', 'ctx'), pairs)]
    pallas_call x4 -> x1, Pallas kernels: 42.9 us -> 121 us  [gather_call(): pl.pallas_call(gather_kernel, in_specs=[anywhere] * 8, out_specs=[anywher...]
    unnamed x143 -> x133, local copies, waits for them, and re-layouts: 31.7 us -> 13.9 us
    ppermute x64 -> x37, starting transfers between devices: 117 us -> 102 us  [plane(): return lax.ppermute(arr, ('fsdp', 'ctx'), pairs)]
    ppermute x15, waiting for transfers between devices: 58.7 us -> 67.5 us  [along_z(): return lax.ppermute(arr, 'tp', [(i, (i + dz) % 4) for i in range(4)])]
  transfers between devices with their start and end apart: 81 -> 53, of which waited for: 28 -> 15; matrix products, arithmetic and copies ran while one was open for 13% -> 8% of each run, Pallas kernels for 26% -> 24%
where the time goes in v2:
time: 608 us; the launch traced here: 597 us
  Pallas kernels  292 us (48%)
  starting transfers between devices  122 us (20%)
  waiting for transfers between devices  112 us (18%)
  other arithmetic  41.4 us (7%)
  local copies, waits for them, and re-layouts  27.8 us (5%)
    pallas_call x1, Pallas kernels, gather_call(): pl.pallas_call(gather_kernel, in_specs=[anywhere] * 8, out_specs=[anywher...  121 us
    ppermute x37, starting transfers between devices, plane(): return lax.ppermute(arr, ('fsdp', 'ctx'), pairs)  102 us
    pallas_call x30, Pallas kernels, block(): pl.pallas_call(weight_grad_kernel, grid=(m,), in_specs=[pl.BlockSpec((BLK...  88.2 us
    ppermute x15, waiting for transfers between devices, along_z(): return lax.ppermute(arr, 'tp', [(i, (i + dz) % 4) for i in range(4)])  67.5 us
    ppermute x37, waiting for transfers between devices, plane(): return lax.ppermute(arr, ('fsdp', 'ctx'), pairs)  44.1 us
    pallas_call x4, Pallas kernels, two_products(): pl.pallas_call(two_products_kernel, grid_spec=pltpu.PrefetchScalarGridSpe...  40.5 us
    pallas_call x1, Pallas kernels, attention(): pl.pallas_call(attention_kernel, grid_spec=pltpu.PrefetchScalarGridSpec(n...  25.9 us
    ppermute x15, starting transfers between devices, along_z(): return lax.ppermute(arr, 'tp', [(i, (i + dz) % 4) for i in range(4)])  18.3 us
  transfers between devices with their start and end apart: 53, of which 15 were waited for; matrix products, arithmetic and copies ran while one was open for 8% of the time, Pallas kernels for 24%

profile of v2, /device:TPU:1, one launch (start us, length us, event | category | flops | bytes accessed | tf_op | source)
XLA Modules:
  0.0 596.9 jit_solution(805009236828476750)
XLA Ops:
  7.1 8.9 %fusion.1 = (f32[1024,256]{1,0:T(8,128)}, f32[1024,256]{1,0:T(8,128)}, f32[1024,256]{1,0:T(8,128)}, f32[1024,256]{1,0:T(8,128)}) fusion(f32[1024]{0:T(1024)S(1)} %get-tuple-element.143, f32[256]{0:T(256)S(1)} %get-tuple-element.141, f32[256]{0:T(256)S(1)} %get-tuple-element.142, f32[1024]{0:T(1024)S(1)} %get-tuple-element.144), kind=kLoop, calls=%fused_computation.10 | loop fusion | flops 1048576 | bytes 4204544 | tf_op jit(solution)/shard_map/mul | solution.py:681
  16.7 121.3 %gather_phase.1 = (bf16[2048,1024]{1,0:T(8,128)(2,1)}, bf16[2048,1024]{1,0:T(8,128)(2,1)}, bf16[2048,1024]{1,0:T(8,128)(2,1)}, bf16[2048,1024]{1,0:T(8,128)(2,1)...) custom-call(bf16[256,1024]{1,0:T(8,128)(2,1)} %get-tuple-element.145, ...), custom_call_target="tpu_custom_call" | custom-call | flops 12884901888 | bytes 67108864 | tf_op jit(solution)/shard_map/gather_phase/pallas_call | solution.py:627
  138.0 25.9 %attention.1 = (bf16[1024,256]{1,0:T(8,128)(2,1)}, bf16[1024,256]{1,0:T(8,128)(2,1)}, f32[1024,512]{1,0:T(8,128)}, bf16[1024,512]{1,0:T(8,128)(2,1)}) custom-call(s32[5]{0:T(128)} %stack.50.place, bf16[1024,256]{1,0:T(8,128)(2,1)} %get-tuple-element.32.q, bf16[1024,512]{1,0:T(8,128)(2,1)} %get-tuple-element.33.kv, bf16[1024,512]{1,0:T(8,128)(2,1)} %get-tuple-element.34.kvr, ...), custom_call_target="tpu_custom_call" | custom-call | flops 19327352832 | bytes 12582912 | tf_op jit(solution)/shard_map/attention/pallas_call | solution.py:215
  165.1 3.3 weight_grad.51
  168.9 3.3 weight_grad.52
  174.4 3.3 weight_grad.53
  178.3 3.3 weight_grad.47
  182.4 3.3 weight_grad.56
  185.7 3.3 weight_grad.57
  189.0 3.3 weight_grad.59
  192.3 3.3 weight_grad.54
  195.6 3.3 weight_grad.50
  198.9 3.3 weight_grad.48
  202.2 3.3 weight_grad.49
  222.8 3.3 weight_grad.46
  226.0 4.0 weight_grad.55
  230.0 4.0 weight_grad.58
  234.0 9.6 %two_products.4 = bf16[512,2048]{1,0:T(8,128)(2,1)} custom-call(s32[5]{0:T(128)} %stack.50.place, bf16[1024,256]{1,0:T(8,128)(2,1)} %get-tuple-element.36.refs_0_.refs_1_.refs_2_.refs_3_, bf16[1024,256]{1,0:T(8,128)(2,1)} %get-tuple-element.36.refs_0_.refs_1_.refs_2_.refs_3_, bf16[1024,256]{1,0:T(8,128)(2,1)} %get-tuple-element.36.refs_0_.refs_1_.refs_2_.refs_3_, ...), custom_call_target="tpu_custom_call" | custom-call | flops 2684354560 | bytes 8650752 | tf_op jit(solution)/shard_map/two_products/pallas_call | solution.py:304
  247.8 26.9 %collective-permute-start.43 = (bf16[128,1024]{1,0:T(8,128)(2,1)S(1)}, bf16[128,1024]{1,0:T(8,128)(2,1)S(1)}, u32[]{:S(2)}, u32[]{:S(2)}) collective-permute-start(bf16[128,1024]{1,0:T(8,128)(2,1)S(1)} %get-tuple-element.120), channel_id=1, source_target_pairs={{0,24},{4,28},{8,16},{12,20},{16,0},{20,4},{24,8},{28,12},{32,56},... | collective-permute-start | bytes 786440 | tf_op jit(solution)/shard_map/ppermute | solution.py:43
  276.8 9.6 %two_products.5 = bf16[512,2048]{1,0:T(8,128)(2,1)} custom-call(s32[5]{0:T(128)} %stack.50.place, bf16[1024,256]{1,0:T(8,128)(2,1)} %get-tuple-element.36.refs_0_.refs_1_.refs_2_.refs_3_, bf16[1024,256]{1,0:T(8,128)(2,1)} %get-tuple-element.36.refs_0_.refs_1_.refs_2_.refs_3_, bf16[1024,256]{1,0:T(8,128)(2,1)} %get-tuple-element.36.refs_0_.refs_1_.refs_2_.refs_3_, ...), custom_call_target="tpu_custom_call" | custom-call | flops 2684354560 | bytes 8650752 | tf_op jit(solution)/shard_map/two_products/pallas_call | solution.py:304
  293.2 10.7 %two_products.6.b = bf16[512,2048]{1,0:T(8,128)(2,1)} custom-call(s32[5]{0:T(128)} %stack.50.place, bf16[1024,768]{1,0:T(8,128)(2,1)} %pad_maximum_fusion.refs_0_.refs_1_.refs_2_.refs_3_, bf16[1024,768]{1,0:T(8,128)(2,1)} %pad_maximum_fusion.refs_0_.refs_1_.refs_2_.refs_3_, bf16[1024,768]{1,0:T(8,128)(2,1)} %pad_maximum_fusion.refs_0_.refs_1_.refs_2_.refs_3_, ...), custom_call_target="tpu_custom_call" | custom-call | flops 3758096384 | bytes 11272192 | tf_op jit(solution)/shard_map/two_products/pallas_call | solution.py:304
  303.9 10.6 %two_products.7.a = bf16[512,2048]{1,0:T(8,128)(2,1)} custom-call(s32[5]{0:T(128)} %stack.50.place, bf16[1024,768]{1,0:T(8,128)(2,1)} %pad_maximum_fusion.refs_0_.refs_1_.refs_2_.refs_3_, bf16[1024,768]{1,0:T(8,128)(2,1)} %pad_maximum_fusion.refs_0_.refs_1_.refs_2_.refs_3_, bf16[1024,768]{1,0:T(8,128)(2,1)} %pad_maximum_fusion.refs_0_.refs_1_.refs_2_.refs_3_, ...), custom_call_target="tpu_custom_call" | custom-call | flops 3758096384 | bytes 11272192 | tf_op jit(solution)/shard_map/two_products/pallas_call | solution.py:304
  314.5 7.7 %gain_grads.1 = (f32[1,2048]{1,0:T(1,128)}, f32[1,2048]{1,0:T(1,128)}) custom-call(s32[5]{0:T(128)} %stack.50.place, bf16[512,2048]{1,0:T(8,128)(2,1)} %two_products.7.a, bf16[512,2048]{1,0:T(8,128)(2,1)} %two_products.6.b, bf16[1024,2048]{1,0:T(8,128)(2,1)} %get-tuple-element.46.refs_0_.refs_1_.refs_2_.refs_3_.refs_4_.refs_5_.refs_6_.refs_7_, ...), custom_call_target="tpu_custom_call" | custom-call | flops 6291456 | bytes 8388608 | tf_op jit(solution)/shard_map/gain_grads/pallas_call | solution.py:342
  322.9 3.7 collective-permute-start.15
  341.9 3.0 weight_grad.36
  353.4 5.9 collective-permute-start.47
  362.9 6.1 %collective-permute-start.18 = (f32[2,2048]{1,0:T(2,128)S(1)}, f32[2,2048]{1,0:T(2,128)S(1)}, u32[]{:S(2)}, u32[]{:S(2)}) collective-permute-start(f32[2,2048]{1,0:T(2,128)S(1)} %add_add_fusion), channel_id=1, source_target_pairs={{0,4},{4,0},{8,12},{12,8},{16,20},{20,16},{24,28},{28,24},{32,36},... | collective-permute-start | bytes 49160 | tf_op jit(solution)/shard_map/ppermute | solution.py:43
  370.1 3.2 collective-permute-start.19
  381.9 3.0 weight_grad.30
  388.6 3.5 collective-permute-start.35
  403.2 5.9 collective-permute-done.30
  412.4 10.7 %collective-permute-done.49 = bf16[256,1024]{1,0:T(8,128)(2,1)S(1)} collective-permute-done((bf16[256,1024]{1,0:T(8,128)(2,1)}, bf16[256,1024]{1,0:T(8,128)(2,1)S(1)}, u32[]{:S(2)}, u32[]{:S(2)}) %collective-permute-start.49) | collective-permute-done | bytes 524320 | tf_op jit(solution)/shard_map/ppermute | solution.py:43
  424.7 11.9 %collective-permute-start.45 = (bf16[256,1024]{1,0:T(8,128)(2,1)S(1)}, bf16[256,1024]{1,0:T(8,128)(2,1)S(1)}, u32[]{:S(2)}, u32[]{:S(2)}) collective-permute-start(bf16[256,1024]{1,0:T(8,128)(2,1)S(1)} %add_convert_fusion.6), channel_id=1, source_target_pairs={{0,4},{4,0},{8,12},{12,8},{16,20},{20,16},{24,28},{28,24},{32,36},... | collective-permute-start | bytes 1572872 | tf_op jit(solution)/shard_map/ppermute | solution.py:43
  436.7 8.8 %collective-permute-done.26 = bf16[256,1024]{1,0:T(8,128)(2,1)S(1)} collective-permute-done((bf16[256,1024]{1,0:T(8,128)(2,1)}, bf16[256,1024]{1,0:T(8,128)(2,1)S(1)}, u32[]{:S(2)}, u32[]{:S(2)}) %collective-permute-start.26) | collective-permute-done | bytes 524320 | tf_op jit(solution)/shard_map/ppermute | solution.py:43
  447.2 12.6 %collective-permute-start.8 = (bf16[512,2048]{1,0:T(8,128)(2,1)}, bf16[512,2048]{1,0:T(8,128)(2,1)}, u32[]{:S(2)}, u32[]{:S(2)}) collective-permute-start(bf16[512,2048]{1,0:T(8,128)(2,1)} %two_products.7.a), channel_id=1, source_target_pairs={{0,4},{4,0},{8,12},{12,8},{16,20},{20,16},{24,28},{28,24},{32,36},... | collective-permute-start | bytes 6291464 | tf_op jit(solution)/shard_map/ppermute | solution.py:43
  463.5 11.3 %collective-permute-done.51 = bf16[256,1024]{1,0:T(8,128)(2,1)S(1)} collective-permute-done((bf16[256,1024]{1,0:T(8,128)(2,1)S(1)}, bf16[256,1024]{1,0:T(8,128)(2,1)S(1)}, u32[]{:S(2)}, u32[]{:S(2)}) %collective-permute-start.51) | collective-permute-done | bytes 524320 | tf_op jit(solution)/shard_map/ppermute | solution.py:43
  476.5 3.1 add_convert_fusion.16
  480.5 5.5 collective-permute-done.33
  487.8 17.7 %collective-permute-done.1.p1 = bf16[128,2048]{1,0:T(8,128)(2,1)S(1)} collective-permute-done((bf16[128,2048]{1,0:T(8,128)(2,1)S(1)}, bf16[128,2048]{1,0:T(8,128)(2,1)S(1)}, u32[]{:S(2)}, u32[]{:S(2)}) %collective-permute-start.1) | collective-permute-done | bytes 524320 | tf_op jit(solution)/shard_map/ppermute | solution.py:56
  507.3 3.9 forward_rows.1
  522.0 3.2 copy.58
  525.2 3.2 add_convert_fusion.12
  535.1 15.4 %collective-permute-done.10.p2 = bf16[128,2048]{1,0:T(8,128)(2,1)S(1)} collective-permute-done((bf16[128,2048]{1,0:T(8,128)(2,1)S(1)}, bf16[128,2048]{1,0:T(8,128)(2,1)S(1)}, u32[]{:S(2)}, u32[]{:S(2)}) %collective-permute-start.10) | collective-permute-done | bytes 524320 | tf_op jit(solution)/shard_map/ppermute | solution.py:56
  550.5 7.8 %collective-permute-done.11.p3 = bf16[128,2048]{1,0:T(8,128)(2,1)S(1)} collective-permute-done((bf16[128,2048]{1,0:T(8,128)(2,1)S(1)}, bf16[128,2048]{1,0:T(8,128)(2,1)S(1)}, u32[]{:S(2)}, u32[]{:S(2)}) %collective-permute-start.11) | collective-permute-done | bytes 524320 | tf_op jit(solution)/shard_map/ppermute | solution.py:56
  561.1 4.5 backward_rows.1
  570.5 6.4 %collective-permute-done.12 = bf16[128,2048]{1,0:T(8,128)(2,1)S(1)} collective-permute-done((bf16[128,2048]{1,0:T(8,128)(2,1)}, bf16[128,2048]{1,0:T(8,128)(2,1)S(1)}, u32[]{:S(2)}, u32[]{:S(2)}) %collective-permute-start.12) | collective-permute-done | bytes 524320 | tf_op jit(solution)/shard_map/ppermute | solution.py:56
  576.9 4.0 collective-permute-done.13
  581.0 14.1 %collective-permute-done.14 = bf16[128,2048]{1,0:T(8,128)(2,1)S(1)} collective-permute-done((bf16[128,2048]{1,0:T(8,128)(2,1)}, bf16[128,2048]{1,0:T(8,128)(2,1)S(1)}, u32[]{:S(2)}, u32[]{:S(2)}) %collective-permute-start.14) | collective-permute-done | bytes 524320 | tf_op jit(solution)/shard_map/ppermute | solution.py:56
  (339 shorter events, 137.6 us)
Async XLA Ops:
  163.8 126.4 %collective-permute-start.7 = (bf16[1024,512]{1,0:T(8,128)(2,1)}, bf16[1024,512]{1,0:T(8,128)(2,1)}, u32[]{:S(2)}, u32[]{:S(2)}) collective-permute-start(bf16[1024,512]{1,0:T(8,128)(2,1)} %get-tuple-element.43), channel_id=1, source_target_pairs={{8,0},{12,4},{24,16},{28,20},{40,32},{44,36},{56,48},{60,52},{72,6... | collective-permute-start | bytes 3145736 | tf_op jit(solution)/shard_map/ppermute | solution.py:52
  168.4 75.3 %collective-permute-start.39 = (bf16[256,1024]{1,0:T(8,128)(2,1)}, bf16[256,1024]{1,0:T(8,128)(2,1)S(1)}, u32[]{:S(2)}, u32[]{:S(2)}) collective-permute-start(bf16[256,1024]{1,0:T(8,128)(2,1)} %weight_grad.51), channel_id=1, source_target_pairs={{0,32},{4,36},{8,40},{12,44},{16,48},{20,52},{24,56},{28,60},{32,6... | collective-permute-start | bytes 1572872 | tf_op jit(solution)/shard_map/ppermute | solution.py:43
  172.2 73.8 %collective-permute-start.40 = (bf16[256,1024]{1,0:T(8,128)(2,1)}, bf16[256,1024]{1,0:T(8,128)(2,1)S(1)}, u32[]{:S(2)}, u32[]{:S(2)}) collective-permute-start(bf16[256,1024]{1,0:T(8,128)(2,1)} %weight_grad.52), channel_id=1, source_target_pairs={{0,96},{4,100},{8,104},{12,108},{16,112},{20,116},{24,120},{28,124... | collective-permute-start | bytes 1572872 | tf_op jit(solution)/shard_map/ppermute | solution.py:43
  177.7 69.5 %collective-permute-start.41 = (bf16[256,1024]{1,0:T(8,128)(2,1)}, bf16[256,1024]{1,0:T(8,128)(2,1)S(1)}, u32[]{:S(2)}, u32[]{:S(2)}) collective-permute-start(bf16[256,1024]{1,0:T(8,128)(2,1)} %weight_grad.53), channel_id=1, source_target_pairs={{0,64},{4,68},{8,72},{12,76},{16,80},{20,84},{24,88},{28,92},{32,9... | collective-permute-start | bytes 1572872 | tf_op jit(solution)/shard_map/ppermute | solution.py:43
  181.6 66.2 %collective-permute-start.36 = (bf16[256,1024]{1,0:T(8,128)(2,1)}, bf16[256,1024]{1,0:T(8,128)(2,1)S(1)}, u32[]{:S(2)}, u32[]{:S(2)}) collective-permute-start(bf16[256,1024]{1,0:T(8,128)(2,1)} %weight_grad.47), channel_id=1, source_target_pairs={{0,32},{4,36},{8,40},{12,44},{16,48},{20,52},{24,56},{28,60},{32,6... | collective-permute-start | bytes 1572872 | tf_op jit(solution)/shard_map/ppermute | solution.py:43
  243.7 42.7 %collective-permute-start.37 = (bf16[256,1024]{1,0:T(8,128)(2,1)S(1)}, bf16[256,1024]{1,0:T(8,128)(2,1)S(1)}, u32[]{:S(2)}, u32[]{:S(2)}) collective-permute-start(bf16[256,1024]{1,0:T(8,128)(2,1)S(1)} %copy-done.41), channel_id=1, source_target_pairs={{0,96},{4,100},{8,104},{12,108},{16,112},{20,116},{24,120},{28,124... | collective-permute-start | bytes 1572872 | tf_op jit(solution)/shard_map/ppermute | solution.py:43
  246.0 40.5 %collective-permute-start.38 = (bf16[256,1024]{1,0:T(8,128)(2,1)S(1)}, bf16[256,1024]{1,0:T(8,128)(2,1)S(1)}, u32[]{:S(2)}, u32[]{:S(2)}) collective-permute-start(bf16[256,1024]{1,0:T(8,128)(2,1)S(1)} %copy-done.40), channel_id=1, source_target_pairs={{0,64},{4,68},{8,72},{12,76},{16,80},{20,84},{24,88},{28,92},{32,9... | collective-permute-start | bytes 1572872 | tf_op jit(solution)/shard_map/ppermute | solution.py:43
  247.5 41.6 %collective-permute-start.42 = (bf16[128,1024]{1,0:T(8,128)(2,1)S(1)}, bf16[128,1024]{1,0:T(8,128)(2,1)S(1)}, u32[]{:S(2)}, u32[]{:S(2)}) collective-permute-start(bf16[128,1024]{1,0:T(8,128)(2,1)S(1)} %get-tuple-element.119), channel_id=1, source_target_pairs={{0,16},{4,20},{8,24},{12,28},{16,8},{20,12},{24,0},{28,4},{32,48},... | collective-permute-start | bytes 786440 | tf_op jit(solution)/shard_map/ppermute | solution.py:43
  247.8 41.4 %collective-permute-start.43 = (bf16[128,1024]{1,0:T(8,128)(2,1)S(1)}, bf16[128,1024]{1,0:T(8,128)(2,1)S(1)}, u32[]{:S(2)}, u32[]{:S(2)}) collective-permute-start(bf16[128,1024]{1,0:T(8,128)(2,1)S(1)} %get-tuple-element.120), channel_id=1, source_target_pairs={{0,24},{4,28},{8,16},{12,20},{16,0},{20,4},{24,8},{28,12},{32,56},... | collective-permute-start | bytes 786440 | tf_op jit(solution)/shard_map/ppermute | solution.py:43
  286.4 62.9 %collective-permute-start.46 = (bf16[512,1024]{1,0:T(8,128)(2,1)S(1)}, bf16[512,1024]{1,0:T(8,128)(2,1)}, u32[]{:S(2)}, u32[]{:S(2)}) collective-permute-start(bf16[512,1024]{1,0:T(8,128)(2,1)S(1)} %copy-done.28), channel_id=1, source_target_pairs={{0,16},{4,20},{8,24},{12,28},{16,8},{20,12},{24,0},{28,4},{32,48},... | collective-permute-start | bytes 3145736 | tf_op jit(solution)/shard_map/ppermute | solution.py:43
  286.5 66.8 %collective-permute-start.48 = (bf16[512,1024]{1,0:T(8,128)(2,1)S(1)}, bf16[512,1024]{1,0:T(8,128)(2,1)}, u32[]{:S(2)}, u32[]{:S(2)}) collective-permute-start(bf16[512,1024]{1,0:T(8,128)(2,1)S(1)} %copy-done.27), channel_id=1, source_target_pairs={{0,24},{4,28},{8,16},{12,20},{16,0},{20,4},{24,8},{28,12},{32,56},... | collective-permute-start | bytes 3145736 | tf_op jit(solution)/shard_map/ppermute | solution.py:43
  289.7 106.3 %collective-permute-start.44 = (bf16[256,1024]{1,0:T(8,128)(2,1)S(1)}, bf16[256,1024]{1,0:T(8,128)(2,1)S(1)}, u32[]{:S(2)}, u32[]{:S(2)}) collective-permute-start(bf16[256,1024]{1,0:T(8,128)(2,1)S(1)} %add_convert_fusion.7), channel_id=1, source_target_pairs={{0,8},{4,12},{8,0},{12,4},{16,24},{20,28},{24,16},{28,20},{32,40},... | collective-permute-start | bytes 1572872 | tf_op jit(solution)/shard_map/ppermute | solution.py:43
  322.9 39.9 %collective-permute-start.15 = (f32[2,2048]{1,0:T(2,128)S(1)}, f32[2,2048]{1,0:T(2,128)S(1)}, u32[]{:S(2)}, u32[]{:S(2)}) collective-permute-start(f32[2,2048]{1,0:T(2,128)S(1)} %pad_maximum_fusion.18), channel_id=1, source_target_pairs={{0,2},{1,3},{2,0},{3,1},{4,6},{5,7},{6,4},{7,5},{8,10},{9,11},{10,... | collective-permute-start | bytes 49160 | tf_op jit(solution)/shard_map/ppermute | solution.py:56
  326.6 36.2 %collective-permute-start.16 = (f32[2,2048]{1,0:T(2,128)S(1)}, f32[2,2048]{1,0:T(2,128)S(1)}, u32[]{:S(2)}, u32[]{:S(2)}) collective-permute-start(f32[2,2048]{1,0:T(2,128)S(1)} %pad_maximum_fusion.18), channel_id=1, source_target_pairs={{0,1},{1,2},{2,3},{3,0},{4,5},{5,6},{6,7},{7,4},{8,9},{9,10},{10,1... | collective-permute-start | bytes 49160 | tf_op jit(solution)/shard_map/ppermute | solution.py:56
  349.3 13.5 %collective-permute-start.17 = (f32[2,2048]{1,0:T(2,128)S(1)}, f32[2,2048]{1,0:T(2,128)S(1)}, u32[]{:S(2)}, u32[]{:S(2)}) collective-permute-start(f32[2,2048]{1,0:T(2,128)S(1)} %pad_maximum_fusion.18), channel_id=1, source_target_pairs={{0,3},{1,0},{2,1},{3,2},{4,7},{5,4},{6,5},{7,6},{8,11},{9,8},{10,9... | collective-permute-start | bytes 49160 | tf_op jit(solution)/shard_map/ppermute | solution.py:56
  353.4 45.9 %collective-permute-start.47 = (bf16[256,1024]{1,0:T(8,128)(2,1)}, bf16[256,1024]{1,0:T(8,128)(2,1)}, u32[]{:S(2)}, u32[]{:S(2)}) collective-permute-start(bf16[256,1024]{1,0:T(8,128)(2,1)} %add_convert_fusion.5), channel_id=1, source_target_pairs={{0,32},{4,36},{8,40},{12,44},{16,48},{20,52},{24,56},{28,60},{32,6... | collective-permute-start | bytes 1572872 | tf_op jit(solution)/shard_map/ppermute | solution.py:43
  362.9 7.0 %collective-permute-start.18 = (f32[2,2048]{1,0:T(2,128)S(1)}, f32[2,2048]{1,0:T(2,128)S(1)}, u32[]{:S(2)}, u32[]{:S(2)}) collective-permute-start(f32[2,2048]{1,0:T(2,128)S(1)} %add_add_fusion), channel_id=1, source_target_pairs={{0,4},{4,0},{8,12},{12,8},{16,20},{20,16},{24,28},{28,24},{32,36},... | collective-permute-start | bytes 49160 | tf_op jit(solution)/shard_map/ppermute | solution.py:43
  370.1 8.8 %collective-permute-start.19 = (f32[3328]{0:T(1024)S(1)}, f32[3328]{0:T(1024)S(1)}, u32[]{:S(2)}, u32[]{:S(2)}) collective-permute-start(f32[3328]{0:T(1024)S(1)} %get-tuple-element.133), channel_id=1, source_target_pairs={{0,64},{4,68},{8,72},{12,76},{16,80},{20,84},{24,88},{28,92},{32,9... | collective-permute-start | bytes 39944 | tf_op jit(solution)/shard_map/ppermute | solution.py:43
  379.7 8.9 %collective-permute-start.24 = (f32[2560]{0:T(1024)S(1)}, f32[2560]{0:T(1024)S(1)}, u32[]{:S(2)}, u32[]{:S(2)}) collective-permute-start(f32[2560]{0:T(1024)S(1)} %get-tuple-element.131), channel_id=1, source_target_pairs={{0,24},{4,28},{8,16},{12,20},{16,0},{20,4},{24,8},{28,12},{32,56},... | collective-permute-start | bytes 30728 | tf_op jit(solution)/shard_map/ppermute | solution.py:43
  385.9 14.3 %collective-permute-start.28 = (bf16[256,1024]{1,0:T(8,128)(2,1)}, bf16[256,1024]{1,0:T(8,128)(2,1)}, u32[]{:S(2)}, u32[]{:S(2)}) collective-permute-start(bf16[256,1024]{1,0:T(8,128)(2,1)} %pad_maximum_fusion.5), channel_id=1, source_target_pairs={{0,32},{4,36},{8,40},{12,44},{16,48},{20,52},{24,56},{28,60},{32,6... | collective-permute-start | bytes 1572872 | tf_op jit(solution)/shard_map/ppermute | solution.py:43
  385.9 16.5 %collective-permute-start.29 = (bf16[256,1024]{1,0:T(8,128)(2,1)}, bf16[256,1024]{1,0:T(8,128)(2,1)}, u32[]{:S(2)}, u32[]{:S(2)}) collective-permute-start(bf16[256,1024]{1,0:T(8,128)(2,1)} %pad_maximum_fusion.6), channel_id=1, source_target_pairs={{0,96},{4,100},{8,104},{12,108},{16,112},{20,116},{24,120},{28,124... | collective-permute-start | bytes 1572872 | tf_op jit(solution)/shard_map/ppermute | solution.py:43
  393.0 16.1 %collective-permute-start.30 = (bf16[256,1024]{1,0:T(8,128)(2,1)}, bf16[256,1024]{1,0:T(8,128)(2,1)}, u32[]{:S(2)}, u32[]{:S(2)}) collective-permute-start(bf16[256,1024]{1,0:T(8,128)(2,1)} %pad_maximum_fusion.7), channel_id=1, source_target_pairs={{0,64},{4,68},{8,72},{12,76},{16,80},{20,84},{24,88},{28,92},{32,9... | collective-permute-start | bytes 1572872 | tf_op jit(solution)/shard_map/ppermute | solution.py:43
  396.0 80.5 %collective-permute-start = (bf16[512,2048]{1,0:T(8,128)(2,1)S(1)}, bf16[512,2048]{1,0:T(8,128)(2,1)}, u32[]{:S(2)}, u32[]{:S(2)}) collective-permute-start(bf16[512,2048]{1,0:T(8,128)(2,1)S(1)} %copy-done.4), channel_id=1, source_target_pairs={{0,4},{4,0},{8,12},{12,8},{16,20},{20,16},{24,28},{28,24},{32,36},... | collective-permute-start | bytes 6291464 | tf_op jit(solution)/shard_map/ppermute | solution.py:43
  399.2 23.8 %collective-permute-start.49 = (bf16[256,1024]{1,0:T(8,128)(2,1)}, bf16[256,1024]{1,0:T(8,128)(2,1)S(1)}, u32[]{:S(2)}, u32[]{:S(2)}) collective-permute-start(bf16[256,1024]{1,0:T(8,128)(2,1)} %get-tuple-element.113), channel_id=1, source_target_pairs={{0,96},{4,100},{8,104},{12,108},{16,112},{20,116},{24,120},{28,124... | collective-permute-start | bytes 1572872 | tf_op jit(solution)/shard_map/ppermute | solution.py:43
  400.2 24.5 %collective-permute-start.50 = (bf16[256,1024]{1,0:T(8,128)(2,1)}, bf16[256,1024]{1,0:T(8,128)(2,1)S(1)}, u32[]{:S(2)}, u32[]{:S(2)}) collective-permute-start(bf16[256,1024]{1,0:T(8,128)(2,1)} %get-tuple-element.114), channel_id=1, source_target_pairs={{0,64},{4,68},{8,72},{12,76},{16,80},{20,84},{24,88},{28,92},{32,9... | collective-permute-start | bytes 1572872 | tf_op jit(solution)/shard_map/ppermute | solution.py:43
  402.4 34.3 %collective-permute-start.25 = (bf16[256,1024]{1,0:T(8,128)(2,1)}, bf16[256,1024]{1,0:T(8,128)(2,1)S(1)}, u32[]{:S(2)}, u32[]{:S(2)}) collective-permute-start(bf16[256,1024]{1,0:T(8,128)(2,1)} %pad_maximum_fusion.2), channel_id=1, source_target_pairs={{0,32},{4,36},{8,40},{12,44},{16,48},{20,52},{24,56},{28,60},{32,6... | collective-permute-start | bytes 1572872 | tf_op jit(solution)/shard_map/ppermute | solution.py:43
  409.0 36.5 %collective-permute-start.26 = (bf16[256,1024]{1,0:T(8,128)(2,1)}, bf16[256,1024]{1,0:T(8,128)(2,1)S(1)}, u32[]{:S(2)}, u32[]{:S(2)}) collective-permute-start(bf16[256,1024]{1,0:T(8,128)(2,1)} %pad_maximum_fusion.3), channel_id=1, source_target_pairs={{0,96},{4,100},{8,104},{12,108},{16,112},{20,116},{24,120},{28,124... | collective-permute-start | bytes 1572872 | tf_op jit(solution)/shard_map/ppermute | solution.py:43
  423.1 24.1 %collective-permute-start.27 = (bf16[256,1024]{1,0:T(8,128)(2,1)S(1)}, bf16[256,1024]{1,0:T(8,128)(2,1)S(1)}, u32[]{:S(2)}, u32[]{:S(2)}) collective-permute-start(bf16[256,1024]{1,0:T(8,128)(2,1)S(1)} %copy-done.33), channel_id=1, source_target_pairs={{0,64},{4,68},{8,72},{12,76},{16,80},{20,84},{24,88},{28,92},{32,9... | collective-permute-start | bytes 1572872 | tf_op jit(solution)/shard_map/ppermute | solution.py:43
  424.7 38.6 %collective-permute-start.45 = (bf16[256,1024]{1,0:T(8,128)(2,1)S(1)}, bf16[256,1024]{1,0:T(8,128)(2,1)S(1)}, u32[]{:S(2)}, u32[]{:S(2)}) collective-permute-start(bf16[256,1024]{1,0:T(8,128)(2,1)S(1)} %add_convert_fusion.6), channel_id=1, source_target_pairs={{0,4},{4,0},{8,12},{12,8},{16,20},{20,16},{24,28},{28,24},{32,36},... | collective-permute-start | bytes 1572872 | tf_op jit(solution)/shard_map/ppermute | solution.py:43
  436.7 23.2 %collective-permute-start.31 = (bf16[128,1024]{1,0:T(8,128)(2,1)S(1)}, bf16[128,1024]{1,0:T(8,128)(2,1)S(1)}, u32[]{:S(2)}, u32[]{:S(2)}) collective-permute-start(bf16[128,1024]{1,0:T(8,128)(2,1)S(1)} %get-tuple-element.121), channel_id=1, source_target_pairs={{0,16},{4,20},{8,24},{12,28},{16,8},{20,12},{24,0},{28,4},{32,48},... | collective-permute-start | bytes 786440 | tf_op jit(solution)/shard_map/ppermute | solution.py:43
  445.5 15.3 %collective-permute-start.32 = (bf16[128,1024]{1,0:T(8,128)(2,1)S(1)}, bf16[128,1024]{1,0:T(8,128)(2,1)S(1)}, u32[]{:S(2)}, u32[]{:S(2)}) collective-permute-start(bf16[128,1024]{1,0:T(8,128)(2,1)S(1)} %get-tuple-element.122), channel_id=1, source_target_pairs={{0,24},{4,28},{8,16},{12,20},{16,0},{20,4},{24,8},{28,12},{32,56},... | collective-permute-start | bytes 786440 | tf_op jit(solution)/shard_map/ppermute | solution.py:43
  447.2 78.0 %collective-permute-start.8 = (bf16[512,2048]{1,0:T(8,128)(2,1)}, bf16[512,2048]{1,0:T(8,128)(2,1)}, u32[]{:S(2)}, u32[]{:S(2)}) collective-permute-start(bf16[512,2048]{1,0:T(8,128)(2,1)} %two_products.7.a), channel_id=1, source_target_pairs={{0,4},{4,0},{8,12},{12,8},{16,20},{20,16},{24,28},{28,24},{32,36},... | collective-permute-start | bytes 6291464 | tf_op jit(solution)/shard_map/ppermute | solution.py:43
  459.8 15.0 %collective-permute-start.51 = (bf16[256,1024]{1,0:T(8,128)(2,1)S(1)}, bf16[256,1024]{1,0:T(8,128)(2,1)S(1)}, u32[]{:S(2)}, u32[]{:S(2)}) collective-permute-start(bf16[256,1024]{1,0:T(8,128)(2,1)S(1)} %add_convert_fusion.2), channel_id=1, source_target_pairs={{0,8},{4,12},{8,0},{12,4},{16,24},{20,28},{24,16},{28,20},{32,40},... | collective-permute-start | bytes 1572872 | tf_op jit(solution)/shard_map/ppermute | solution.py:43
  461.3 24.8 %collective-permute-start.33 = (bf16[256,1024]{1,0:T(8,128)(2,1)S(1)}, bf16[256,1024]{1,0:T(8,128)(2,1)S(1)}, u32[]{:S(2)}, u32[]{:S(2)}) collective-permute-start(bf16[256,1024]{1,0:T(8,128)(2,1)S(1)} %add_convert_fusion.10), channel_id=1, source_target_pairs={{0,8},{4,12},{8,0},{12,4},{16,24},{20,28},{24,16},{28,20},{32,40},... | collective-permute-start | bytes 1572872 | tf_op jit(solution)/shard_map/ppermute | solution.py:43
  475.0 38.5 %collective-permute-start.52 = (bf16[256,1024]{1,0:T(8,128)(2,1)S(1)}, bf16[256,1024]{1,0:T(8,128)(2,1)S(1)}, u32[]{:S(2)}, u32[]{:S(2)}) collective-permute-start(bf16[256,1024]{1,0:T(8,128)(2,1)S(1)} %add_convert_fusion.1), channel_id=1, source_target_pairs={{0,4},{4,0},{8,12},{12,8},{16,20},{20,16},{24,28},{28,24},{32,36},... | collective-permute-start | bytes 1572872 | tf_op jit(solution)/shard_map/ppermute | solution.py:43
  479.6 26.0 %collective-permute-start.1 = (bf16[128,2048]{1,0:T(8,128)(2,1)S(1)}, bf16[128,2048]{1,0:T(8,128)(2,1)S(1)}, u32[]{:S(2)}, u32[]{:S(2)}) collective-permute-start(bf16[128,2048]{1,0:T(8,128)(2,1)S(1)} %get-tuple-element.109), channel_id=1, source_target_pairs={{0,1},{1,2},{2,3},{3,0},{4,5},{5,6},{6,7},{7,4},{8,9},{9,10},{10,1... | collective-permute-start | bytes 1572872 | tf_op jit(solution)/shard_map/ppermute | solution.py:56
  479.6 26.8 %collective-permute-start.2 = (bf16[128,2048]{1,0:T(8,128)(2,1)S(1)}, bf16[128,2048]{1,0:T(8,128)(2,1)S(1)}, u32[]{:S(2)}, u32[]{:S(2)}) collective-permute-start(bf16[128,2048]{1,0:T(8,128)(2,1)S(1)} %get-tuple-element.108), channel_id=1, source_target_pairs={{0,2},{1,3},{2,0},{3,1},{4,6},{5,7},{6,4},{7,5},{8,10},{9,11},{10,... | collective-permute-start | bytes 1572872 | tf_op jit(solution)/shard_map/ppermute | solution.py:56
  486.1 20.3 %collective-permute-start.3 = (bf16[128,2048]{1,0:T(8,128)(2,1)S(1)}, bf16[128,2048]{1,0:T(8,128)(2,1)S(1)}, u32[]{:S(2)}, u32[]{:S(2)}) collective-permute-start(bf16[128,2048]{1,0:T(8,128)(2,1)S(1)} %get-tuple-element.107), channel_id=1, source_target_pairs={{0,3},{1,0},{2,1},{3,2},{4,7},{5,4},{6,5},{7,6},{8,11},{9,8},{10,9... | collective-permute-start | bytes 1572872 | tf_op jit(solution)/shard_map/ppermute | solution.py:56
  505.5 12.1 %collective-permute-start.34 = (bf16[1,256,1024]{2,1,0:T(8,128)(2,1)S(1)}, bf16[1,256,1024]{2,1,0:T(8,128)(2,1)}, u32[]{:S(2)}, u32[]{:S(2)}) collective-permute-start(bf16[1,256,1024]{2,1,0:T(8,128)(2,1)S(1)} %fusion.4), channel_id=1, source_target_pairs={{0,4},{4,0},{8,12},{12,8},{16,20},{20,16},{24,28},{28,24},{32,36},... | collective-permute-start | bytes 1572872 | tf_op jit(solution)/shard_map/ppermute | solution.py:43
  511.2 21.6 %collective-permute-start.4 = (bf16[128,2048]{1,0:T(8,128)(2,1)}, bf16[128,2048]{1,0:T(8,128)(2,1)}, u32[]{:S(2)}, u32[]{:S(2)}) collective-permute-start(bf16[128,2048]{1,0:T(8,128)(2,1)} %forward_rows.1), channel_id=1, source_target_pairs={{0,3},{1,0},{2,1},{3,2},{4,7},{5,4},{6,5},{7,6},{8,11},{9,8},{10,9... | collective-permute-start | bytes 1572872 | tf_op jit(solution)/shard_map/ppermute | solution.py:56
  513.5 20.5 %collective-permute-start.5 = (bf16[128,2048]{1,0:T(8,128)(2,1)}, bf16[128,2048]{1,0:T(8,128)(2,1)}, u32[]{:S(2)}, u32[]{:S(2)}) collective-permute-start(bf16[128,2048]{1,0:T(8,128)(2,1)} %forward_rows.1), channel_id=1, source_target_pairs={{0,2},{1,3},{2,0},{3,1},{4,6},{5,7},{6,4},{7,5},{8,10},{9,11},{10,... | collective-permute-start | bytes 1572872 | tf_op jit(solution)/shard_map/ppermute | solution.py:56
  513.5 53.6 %collective-permute-start.6 = (bf16[128,2048]{1,0:T(8,128)(2,1)}, bf16[128,2048]{1,0:T(8,128)(2,1)}, u32[]{:S(2)}, u32[]{:S(2)}) collective-permute-start(bf16[128,2048]{1,0:T(8,128)(2,1)} %forward_rows.1), channel_id=1, source_target_pairs={{0,1},{1,2},{2,3},{3,0},{4,5},{5,6},{6,7},{7,4},{8,9},{9,10},{10,1... | collective-permute-start | bytes 1572872 | tf_op jit(solution)/shard_map/ppermute | solution.py:56
  528.4 22.1 %collective-permute-start.10 = (bf16[128,2048]{1,0:T(8,128)(2,1)S(1)}, bf16[128,2048]{1,0:T(8,128)(2,1)S(1)}, u32[]{:S(2)}, u32[]{:S(2)}) collective-permute-start(bf16[128,2048]{1,0:T(8,128)(2,1)S(1)} %get-tuple-element.104), channel_id=1, source_target_pairs={{0,2},{1,3},{2,0},{3,1},{4,6},{5,7},{6,4},{7,5},{8,10},{9,11},{10,... | collective-permute-start | bytes 1572872 | tf_op jit(solution)/shard_map/ppermute | solution.py:56
  530.8 27.4 %collective-permute-start.11 = (bf16[128,2048]{1,0:T(8,128)(2,1)S(1)}, bf16[128,2048]{1,0:T(8,128)(2,1)S(1)}, u32[]{:S(2)}, u32[]{:S(2)}) collective-permute-start(bf16[128,2048]{1,0:T(8,128)(2,1)S(1)} %get-tuple-element.103), channel_id=1, source_target_pairs={{0,3},{1,0},{2,1},{3,2},{4,7},{5,4},{6,5},{7,6},{8,11},{9,8},{10,9... | collective-permute-start | bytes 1572872 | tf_op jit(solution)/shard_map/ppermute | solution.py:56
  532.9 27.5 %collective-permute-start.9 = (bf16[128,2048]{1,0:T(8,128)(2,1)S(1)}, bf16[128,2048]{1,0:T(8,128)(2,1)S(1)}, u32[]{:S(2)}, u32[]{:S(2)}) collective-permute-start(bf16[128,2048]{1,0:T(8,128)(2,1)S(1)} %get-tuple-element.105), channel_id=1, source_target_pairs={{0,1},{1,2},{2,3},{3,0},{4,5},{5,6},{6,7},{7,4},{8,9},{9,10},{10,1... | collective-permute-start | bytes 1572872 | tf_op jit(solution)/shard_map/ppermute | solution.py:56
  565.6 11.2 %collective-permute-start.12 = (bf16[128,2048]{1,0:T(8,128)(2,1)}, bf16[128,2048]{1,0:T(8,128)(2,1)S(1)}, u32[]{:S(2)}, u32[]{:S(2)}) collective-permute-start(bf16[128,2048]{1,0:T(8,128)(2,1)} %backward_rows.1), channel_id=1, source_target_pairs={{0,3},{1,0},{2,1},{3,2},{4,7},{5,4},{6,5},{7,6},{8,11},{9,8},{10,9... | collective-permute-start | bytes 1572872 | tf_op jit(solution)/shard_map/ppermute | solution.py:56
  568.2 12.7 %collective-permute-start.13 = (bf16[128,2048]{1,0:T(8,128)(2,1)}, bf16[128,2048]{1,0:T(8,128)(2,1)S(1)}, u32[]{:S(2)}, u32[]{:S(2)}) collective-permute-start(bf16[128,2048]{1,0:T(8,128)(2,1)} %backward_rows.1), channel_id=1, source_target_pairs={{0,2},{1,3},{2,0},{3,1},{4,6},{5,7},{6,4},{7,5},{8,10},{9,11},{10,... | collective-permute-start | bytes 1572872 | tf_op jit(solution)/shard_map/ppermute | solution.py:56
  569.4 25.7 %collective-permute-start.14 = (bf16[128,2048]{1,0:T(8,128)(2,1)}, bf16[128,2048]{1,0:T(8,128)(2,1)S(1)}, u32[]{:S(2)}, u32[]{:S(2)}) collective-permute-start(bf16[128,2048]{1,0:T(8,128)(2,1)} %backward_rows.1), channel_id=1, source_target_pairs={{0,1},{1,2},{2,3},{3,0},{4,5},{5,6},{6,7},{7,4},{8,9},{9,10},{10,1... | collective-permute-start | bytes 1572872 | tf_op jit(solution)/shard_map/ppermute | solution.py:56
  (64 other events, 520.9 us)
